TPU v7x, 128 devices: a whole 4x4x4 slice. The times are simulated.
128 devices in a mesh: dp: 8 (over z, core), ctx: 16 (over x, y).
Axes of the slice: x: 4, y: 4, z: 4, core: 2. Of those that a mesh axis runs over, the one named last changes fastest.
Arguments:
- ssm_input: bfloat16 [32768, 8192], P(('dp', 'ctx')), may hold values from -6 to 6
- gate_input: bfloat16 [32768, 8192], P(('dp', 'ctx')), may hold values from -6 to 6
- write_basis: bfloat16 [32768, 1024], P(('dp', 'ctx')), may hold values from -2.5 to 2.5
- read_basis: bfloat16 [32768, 1024], P(('dp', 'ctx')), may hold values from -2.5 to 2.5
- step_size: bfloat16 [32768, 128], P(('dp', 'ctx')), may hold values from 0.01 to 0.5, as said below
- decay_rate: float32 [128], replicated, may hold values from 0.001 to 0.35, as said below
- skip_weight: float32 [128], replicated, may hold values from 0.5 to 1.5
- norm_gain: float32 [8192], replicated, may hold values from 0.1 to 1.9
- row_owner: int32 [32768, 1], P(('dp', 'ctx')), may hold values from 0 to 7; in each aligned block of 256 rows (0 to 255, 256 to 511, ...) at most 64 rows name the same one
- document_lengths: int32 [8, 8], P('dp'), may hold values from 1 to 4096, 8192 in all within a row
Outputs:
- layer_output: bfloat16 [32768, 8192], P(('dp', 'ctx'))
Inputs may be any that keep to these rules, and one draw needn't show every extreme that they name: `row_owner`: within each device's block of 256 consecutive rows, no owner is named by more than 64 rows, a bound that some block reaches. `document_lengths`: each row sums to 8192; the largest entry of each row is 4096. `step_size`: Positive. `decay_rate`: Positive.
All inputs are finite; a program needn't handle non-finite values.
Results may differ from a plain program's by a relative error of at most 0.006.
Values may be sent and summed in bfloat16 or wider, within the bound.
A program may use at most 384 MiB of HBM per device.

v0:
```python
import jax
import jax.numpy as jnp
from jax import lax
from jax.sharding import PartitionSpec as P

GROUPS = 8
BLOCK = 512


EPSILON = 1e-05


def entering(value, axis, combine, identity):
    size, position = (lax.axis_size(axis), lax.axis_index(axis))
    everything = jax.tree.map(lambda part: lax.all_gather(part, axis), value)
    start = jax.tree.map(
        lambda part, zero: jnp.broadcast_to(jnp.asarray(zero, part.dtype), part.shape),
        value,
        identity,
    )

    def turn(k, before):
        reached = k < position
        new = combine(before, jax.tree.map(lambda part: part[k], everything))
        return jax.tree.map(lambda a, b: jnp.where(reached, a, b), new, before)

    return lax.fori_loop(0, size, turn, start)


def segment_of(positions, lengths):
    starts = jnp.cumsum(lengths) - lengths
    return jnp.sum((positions[:, None] >= starts[None, :]).astype(jnp.int32), axis=1) - 1


def block_setup(step_rows, decay_rate):
    return jnp.cumsum(-decay_rate[None, :] * step_rows.astype(jnp.float32), axis=0)


def block_summary(values, write_rows, step_rows, cumulative, segments, before):
    block_size, head_count = step_rows.shape
    per_group = head_count // GROUPS
    head_width = values.shape[1] // head_count
    keep_end = (segments == segments[-1]).astype(jnp.float32)
    weights = (
        jnp.exp(cumulative[-1][None, :] - cumulative)
        * step_rows.astype(jnp.float32)
        * keep_end[:, None]
    )
    weighted = (
        weights.reshape(block_size, GROUPS, per_group, 1)
        * write_rows.reshape(block_size, GROUPS, 1, -1)
    ).astype(jnp.bfloat16)
    grouped_values = values.reshape(block_size, GROUPS, per_group, head_width)
    state_sum = jnp.einsum(
        "sghp,sghn->ghpn", grouped_values, weighted, preferred_element_type=jnp.float32
    ).reshape(head_count, head_width, -1)
    block_decay = jnp.exp(cumulative[-1]) * (segments[-1] == before).astype(jnp.float32)
    return (block_decay, state_sum)


def block_inner(values, write_rows, read_rows, step_rows, cumulative, segments):
    block_size, head_count = step_rows.shape
    per_group = head_count // GROUPS
    head_width = values.shape[1] // head_count
    slot_order = jnp.arange(block_size)
    allowed = (slot_order[:, None] >= slot_order[None, :]) & (
        segments[:, None] == segments[None, :]
    )
    grouped_values = values.reshape(block_size, GROUPS, per_group, head_width)
    writes_grouped = write_rows.reshape(block_size, GROUPS, -1)
    reads_grouped = read_rows.reshape(block_size, GROUPS, -1)
    step_values = step_rows.astype(jnp.float32)
    inner_parts = []
    for group_index in range(GROUPS):
        head_start = group_index * per_group
        intersection = jnp.dot(
            reads_grouped[:, group_index],
            writes_grouped[:, group_index].T,
            preferred_element_type=jnp.float32,
        )
        local_cum = cumulative[:, head_start : head_start + per_group].T
        exponent = jnp.where(allowed[None], local_cum[:, :, None] - local_cum[:, None, :], -jnp.inf)
        local_steps = step_values[:, head_start : head_start + per_group].T
        scores = (intersection[None] * jnp.exp(exponent) * local_steps[:, None, :]).astype(
            jnp.bfloat16
        )
        inner_parts.append(
            jnp.einsum(
                "hqs,shp->qhp",
                scores,
                grouped_values[:, group_index],
                preferred_element_type=jnp.float32,
            )
        )
    return jnp.stack(inner_parts, axis=1).reshape(block_size, head_count, head_width)


def block_outer(values, read_rows, carried, cumulative, segments, before, skip_weight):
    block_size, head_count = cumulative.shape
    per_group = head_count // GROUPS
    head_width = values.shape[1] // head_count
    factor = jnp.exp(cumulative) * (segments == before).astype(jnp.float32)[:, None]
    rounded_state = carried.astype(jnp.bfloat16).reshape(GROUPS, per_group, head_width, -1)
    carried_part = jnp.einsum(
        "qgn,ghpn->qghp",
        read_rows.reshape(block_size, GROUPS, -1),
        rounded_state,
        preferred_element_type=jnp.float32,
    ).reshape(block_size, head_count, head_width)
    direct = skip_weight[None, :, None] * values.reshape(block_size, head_count, head_width).astype(
        jnp.float32
    )
    return carried_part * factor[:, :, None] + direct


def shards(
    ssm_input,
    gate_input,
    write_basis,
    read_basis,
    step_size,
    decay_rate,
    skip_weight,
    norm_gain,
    row_owner,
    document_lengths,
):
    data_size = lax.axis_size("dp")
    row_count = ssm_input.shape[0]
    capacity = 2 * row_count // data_size
    owners = row_owner[:, 0]
    owner_table = (owners[:, None] == jnp.arange(data_size, dtype=jnp.int32)[None, :]).astype(
        jnp.int32
    )
    owner_rank = jnp.sum((jnp.cumsum(owner_table, axis=0) - 1) * owner_table, axis=1)
    slot_index = owners * capacity + owner_rank

    def pack_slots(values):
        zero_slots = jnp.zeros((data_size * capacity,) + values.shape[1:], values.dtype)
        return (
            zero_slots.at[slot_index].set(values).reshape((data_size, capacity) + values.shape[1:])
        )

    basis_rows = jnp.concatenate([write_basis, read_basis], axis=1)
    received = (
        lax.all_to_all(pack_slots(ssm_input), "dp", split_axis=0, concat_axis=0, tiled=True),
        lax.all_to_all(pack_slots(basis_rows), "dp", split_axis=0, concat_axis=0, tiled=True),
        lax.all_to_all(pack_slots(step_size), "dp", split_axis=0, concat_axis=0, tiled=True),
    )
    slot_count = data_size * capacity
    value_slots = received[0].reshape(slot_count, -1)
    basis_slots = received[1].reshape(slot_count, -1)
    half_width = basis_slots.shape[1] // 2
    write_slots = basis_slots[:, :half_width]
    read_slots = basis_slots[:, half_width:]
    step_slots = received[2].reshape(slot_count, -1)
    head_count = step_slots.shape[1]
    lengths = document_lengths[0]
    offset = lax.axis_index("ctx") * slot_count
    positions = offset + jnp.arange(-1, slot_count, dtype=jnp.int32)
    segments_all = segment_of(positions, lengths)
    number = 0
    slot_start = number * BLOCK
    cumulative = block_setup(step_slots, decay_rate)
    segments = segments_all[slot_start + 1 : slot_start + 1 + BLOCK]
    before = segments_all[slot_start]
    block_decay, state_sum = block_summary(
        value_slots, write_slots, step_slots, cumulative, segments, before
    )
    cumulatives = [cumulative]
    segment_list = [segments]
    befores = [before]
    decays = [block_decay]
    states = [state_sum]
    inner_parts = []
    device_decay = jnp.ones((head_count,), jnp.float32)
    device_state = jnp.zeros_like(states[0])
    number = 0
    device_decay = device_decay * decays[number]
    device_state = decays[number][:, None, None] * device_state + states[number]

    def combine(earlier, later_part):
        return (
            earlier[0] * later_part[0],
            later_part[0][:, None, None] * earlier[1] + later_part[1],
        )

    identity = (jnp.ones_like(device_decay), jnp.zeros_like(device_state))
    incoming = entering((device_decay, device_state), "ctx", combine, identity)[1]
    inner_parts = [
        block_inner(
            value_slots, write_slots, read_slots, step_slots, cumulatives[0], segment_list[0]
        )
    ]
    number = 0
    carried_part = block_outer(
        value_slots,
        read_slots,
        incoming,
        cumulatives[number],
        segment_list[number],
        befores[number],
        skip_weight,
    )
    outputs = (inner_parts[number] + carried_part).reshape(BLOCK, -1).astype(jnp.bfloat16)
    mixed_slots = outputs.reshape(data_size, capacity, -1)
    returned_rows = lax.all_to_all(
        mixed_slots, "dp", split_axis=0, concat_axis=0, tiled=True
    ).reshape(slot_count, -1)
    ssd_rows = returned_rows[slot_index]
    gated_rows = ssd_rows.astype(jnp.float32) * jax.nn.silu(gate_input.astype(jnp.float32))
    grouped = gated_rows.reshape(row_count, GROUPS, -1)
    inverse_rms = lax.rsqrt(jnp.mean(grouped * grouped, axis=2, keepdims=True) + EPSILON)
    return ((grouped * inverse_rms).reshape(row_count, -1) * norm_gain[None, :]).astype(
        jnp.bfloat16
    )


def solution(mesh):
    placed = (
        P(("dp", "ctx"), None),
        P(("dp", "ctx"), None),
        P(("dp", "ctx"), None),
        P(("dp", "ctx"), None),
        P(("dp", "ctx"), None),
        P(),
        P(),
        P(),
        P(("dp", "ctx"), None),
        P("dp", None),
    )
    return jax.shard_map(
        shards, mesh=mesh, in_specs=placed, out_specs=P(("dp", "ctx"), None), check_vma=False
    )
```

profile of v0, /device:TPU:1, one launch (start us, length us, event | category | flops | bytes accessed | tf_op | source)
XLA Modules:
  0.0 914.5 jit_solution(13178511901684352004)
XLA Ops:
  9.5 2.1 scatter_custom_fusion.2
  11.6 6.8 all-to-all-start.2
  18.4 4.4 scatter_custom_fusion.1
  23.7 4.4 all-to-all-start.1
  28.0 12.5 %scatter_custom_fusion = bf16[512,8192]{1,0:T(8,128)(2,1)} fusion(s32[256]{0:T(256)S(1)} %bitcast.260, bf16[256,8192]{1,0:T(8,128)(2,1)} %param.12, bf16[]{:T(256)} %constant.56.clone.1), kind=kCustom, calls=%fused_computation.45 | custom fusion | bytes 8389120 | tf_op jit(solution)/shard_map/scatter | solution.py:141
  40.5 13.9 %all-to-all-done.1 = bf16[8,64,2048]{2,1,0:T(8,128)(2,1)S(1)} async-done(((bf16[8,64,2048]{2,1,0:T(8,128)(2,1)}), bf16[8,64,2048]{2,1,0:T(8,128)(2,1)S(1)}, u32[]{:S(2)}, u32[]{:S(2)}) %all-to-all-start.1) | async-done | bytes 2097184 | tf_op jit(solution)/shard_map/all_to_all | solution.py:147
  54.4 5.8 all-to-all-start
  70.2 83.9 %all-to-all-done = bf16[8,64,8192]{2,1,0:T(8,128)(2,1)} async-done(((bf16[8,64,8192]{2,1,0:T(8,128)(2,1)}), bf16[8,64,8192]{2,1,0:T(8,128)(2,1)}, u32[]{:S(2)}, u32[]{:S(2)}) %all-to-all-start) | async-done | bytes 8388640 | tf_op jit(solution)/shard_map/all_to_all | solution.py:146
  154.1 23.6 %reshape_reshape.2 = bf16[512,8,16,64]{3,2,1,0:T(8,128)(2,1)} reshape(bf16[8,64,8192]{2,1,0:T(8,128)(2,1)} %all-to-all-done) | data formatting | bytes 16777216 | tf_op jit(solution)/shard_map/reshape;reshape | solution.py:69
  177.7 18.4 %copy.249 = bf16[512,8,16,64]{0,3,2,1:T(8,128)(2,1)} copy(bf16[512,8,16,64]{3,2,1,0:T(8,128)(2,1)} %reshape_reshape.2) | data formatting | bytes 16777216 | tf_op jit(solution)/shard_map/reshape;reshape | solution.py:69
  196.0 12.6 %fusion.1 = f32[8,16,64,128]{3,2,1,0:T(8,128)S(1)} fusion(bf16[512,8,16,64]{0,3,2,1:T(8,128)(2,1)} %copy.249, f32[512,8,128]{2,0,1:T(8,128)} %copy.287, f32[512,8,16]{0,2,1:T(8,128)S(1)} %bitcast.253), kind=kOutput, calls=%fused_computation.8 | convolution fusion | flops 1090519040 | bytes 14942208 | tf_op jit(solution)/shard_map/sghp,sghn->ghpn/dot_general | solution.py:54
  208.7 2.3 bitcast_add_fusion.1
  216.1 1.8 slice_bitcast_fusion.16
  219.6 1.7 copy.258
  221.3 1.7 copy.260
  223.0 1.7 copy.262
  224.8 1.7 copy.264
  226.4 1.7 copy.266
  228.1 1.7 copy.268
  235.7 1.7 copy.280
  237.6 11.6 %mul.342 = f32[512,128,64]{2,1,0:T(8,128)} broadcast(f32[512,128]{1,0:T(8,128)S(1)} %copy-done.1), dimensions={0,1} | broadcast | bytes 17039360 | tf_op jit(solution)/shard_map/mul | solution.py:113
  249.2 28.2 %mul.343 = f32[8,64,8192]{2,1,0:T(8,128)} reshape(f32[512,128,64]{2,1,0:T(8,128)} %mul.342) | data formatting | bytes 33554432 | tf_op jit(solution)/shard_map/mul | solution.py:113
  277.4 19.1 %all-gather = f32[16,1,128]{2,1,0:T(1,128)S(1)} all-gather(f32[1,1,128]{2,1,0:T(1,128)S(1)} %get-tuple-element.133), channel_id=1, replica_groups=mesh['dp'=8,'ctx'=16] {'ctx'}, dimensions={0}, use_global_device_ids=true | all-gather | bytes 8704 | tf_op jit(solution)/shard_map/all_gather | solution.py:15
  299.7 8.0 bitcast_dynamic-update-slice_fusion.7
  307.7 6.6 bitcast_dynamic-update-slice_fusion.6
  314.4 6.7 bitcast_dynamic-update-slice_fusion.5
  321.0 6.7 bitcast_dynamic-update-slice_fusion.4
  327.7 7.1 bitcast_dynamic-update-slice_fusion.3
  334.9 6.7 bitcast_dynamic-update-slice_fusion.2
  341.6 6.7 bitcast_dynamic-update-slice_fusion.1
  348.3 6.6 bitcast_dynamic-update-slice_fusion
  354.9 24.6 %reshape.260 = f32[8,64,8192]{1,0,2:T(8,128)} reshape(f32[512,8,16,64]{0,3,2,1:T(8,128)} %bitcast_dynamic-update-slice_fusion) | data formatting | bytes 33554432 | tf_op jit(solution)/shard_map/reshape | solution.py:95
  379.5 25.0 %copy.294 = f32[8,64,8192]{2,1,0:T(8,128)} copy(f32[8,64,8192]{1,0,2:T(8,128)} %reshape.260) | data formatting | bytes 33554432 | tf_op jit(solution)/shard_map/reshape | solution.py:95
  404.5 174.8 %all-gather.3.cloned.1.call-done = f32[16,128,64,128]{3,2,1,0:T(8,128)} async-done(((f32[1,128,64,128]{3,2,1,0:T(8,128)}), f32[16,128,64,128]{3,2,1,0:T(8,128)}) %all-gather.3.cloned.1.call-update) | async-done | bytes 67108880 | tf_op jit(solution)/shard_map/all_gather | solution.py:15
  579.4 96.2 %while.14 = (s32[]{:T(128)}, f32[128,64,128]{2,1,0:T(8,128)}, s32[]{:T(128)}, f32[16,128]{1,0:T(8,128)S(1)}, f32[16,128,64,128]{3,2,1,0:T(8,128)}, /*index=5*/s32[]{:T(128)}, s32[]{:T(128)}) while((s32[]{:T(128)}, f32[128,64,128]{2,1,0:T(8,128)}, s32[]{:T(128)}, f32[16,128]{1,0:T(8,128)S(1)}, f32[16,128,64,128]{3,2,1,0:T(8,128)}, ...), condition=%wide.region_11.12_spmd.clone, body=%wide.region_10.11_spmd.clone.sunk | while | flops 4194308 | bytes 12584553 | solution.py:27
  579.4 4.8 fusion.61
  584.2 6.1 fusion.61
  590.3 6.1 fusion.61
  596.3 6.1 fusion.61
  602.4 6.1 fusion.61
  608.5 6.1 fusion.61
  614.6 6.1 fusion.61
  620.7 6.1 fusion.61
  626.8 6.1 fusion.61
  632.8 6.1 fusion.61
  638.9 6.1 fusion.61
  645.0 6.1 fusion.61
  651.1 6.1 fusion.61
  657.2 6.1 fusion.61
  663.3 6.1 fusion.61
  669.3 6.1 fusion.61
  675.6 2.7 convert_element_type.97
  678.3 8.0 convolution_bitcast_fusion
  686.3 24.7 %reshape.261 = f32[8,64,8192]{1,0,2:T(8,128)} reshape(f32[512,8,16,64]{0,3,2,1:T(8,128)} %convolution_bitcast_fusion) | data formatting | bytes 33554432 | tf_op jit(solution)/shard_map/reshape | solution.py:109
  711.0 24.6 %copy.297 = f32[8,64,8192]{2,1,0:T(8,128)} copy(f32[8,64,8192]{1,0,2:T(8,128)} %reshape.261) | data formatting | bytes 33554432 | tf_op jit(solution)/shard_map/reshape | solution.py:109
  735.5 23.3 %add_convert_fusion = bf16[8,64,8192]{2,1,0:T(8,128)(2,1)} fusion(f32[8,64,8192]{2,1,0:T(8,128)} %copy.294, bf16[8,64,8192]{2,1,0:T(8,128)(2,1)} %all-to-all-done, f32[8,64,8192]{2,1,0:T(8,128)} %copy.297, f32[8,64,8192]{2,1,0:T(8,128)} %mul.343, f32[8192]{0:T(1024)S(1)} %copy-done.4), kind=kLoop, calls=%fused_computation.9 | loop fusion | flops 25165824 | bytes 67141632 | tf_op jit(solution)/shard_map/convert_element_type | solution.py:205
  758.8 5.7 all-to-all-start.3
  764.6 93.9 %all-to-all-done.3 = bf16[8,64,8192]{2,1,0:T(8,128)(2,1)} async-done(((bf16[8,64,8192]{2,1,0:T(8,128)(2,1)}), bf16[8,64,8192]{2,1,0:T(8,128)(2,1)}, u32[]{:S(2)}, u32[]{:S(2)}) %all-to-all-start.3) | async-done | bytes 8388640 | tf_op jit(solution)/shard_map/all_to_all | solution.py:207
  858.4 13.5 %gather_fusion = bf16[256,8192]{1,0:T(8,128)(2,1)} fusion(bf16[512,8192]{1,0:T(8,128)(2,1)} %bitcast.87, s32[1024]{0:T(1024)S(1)} %pad_clamp_fusion), kind=kCustom, calls=%fused_computation | custom fusion | bytes 8389632 | tf_op jit(solution)/shard_map/gather | solution.py:210
  871.9 5.0 fusion.32
  876.8 10.8 %copy.298 = f32[32,8,8,1024]{3,2,1,0:T(8,128)} copy(f32[32,8,8,1024]{3,1,2,0:T(8,128)S(1)} %bitcast.222) | data formatting | bytes 16777216
  887.6 3.8 reduce_sum.32
  892.3 8.7 copy.299
  901.0 6.2 multiply_convert_fusion.10
  (132 shorter events, 29.3 us)
Async XLA Ops:
  9.5 44.9 %copy-start.19 = (s32[256,1]{0,1:T(1,128)}, s32[256,1]{0,1:T(1,128)S(1)}, u32[]{:S(2)}) copy-start(s32[256,1]{0,1:T(1,128)S(1)} %compare_select_fusion) | copy-start | bytes 3076
  11.6 12.1 %all-to-all-start.2 = ((bf16[8,64,128]{2,1,0:T(8,128)(2,1)}), bf16[8,64,128]{2,1,0:T(8,128)(2,1)S(1)}, u32[]{:S(2)}, u32[]{:S(2)}) async-start(bf16[8,64,128]{2,1,0:T(8,128)(2,1)} %bitcast.15), calls=%async_computation.2 | async-start | bytes 262144 | tf_op jit(solution)/shard_map/all_to_all | solution.py:148
  23.7 30.7 %all-to-all-start.1 = ((bf16[8,64,2048]{2,1,0:T(8,128)(2,1)}), bf16[8,64,2048]{2,1,0:T(8,128)(2,1)S(1)}, u32[]{:S(2)}, u32[]{:S(2)}) async-start(bf16[8,64,2048]{2,1,0:T(8,128)(2,1)} %bitcast.248), calls=%async_computation.1 | async-start | bytes 4194304 | tf_op jit(solution)/shard_map/all_to_all | solution.py:147
  54.4 5.8 copy-start.22
  54.4 5.9 copy-start.23
  54.4 99.7 %all-to-all-start = ((bf16[8,64,8192]{2,1,0:T(8,128)(2,1)}), bf16[8,64,8192]{2,1,0:T(8,128)(2,1)}, u32[]{:S(2)}, u32[]{:S(2)}) async-start(bf16[8,64,8192]{2,1,0:T(8,128)(2,1)} %bitcast.219), calls=%async_computation | async-start | bytes 16777216 | tf_op jit(solution)/shard_map/all_to_all | solution.py:146
  60.2 519.1 %all-gather.3.cloned.1.call-start = ((), (), s32[]{:S(2)}) async-start(), calls=%async_computation.4 | async-start | bytes 71303168 | tf_op jit(solution)/shard_map/all_gather | solution.py:15
  177.7 18.4 %copy-start.3 = (f32[512,128]{0,1:T(8,128)S(1)}, f32[512,128]{0,1:T(8,128)}, u32[]{:S(2)}) copy-start(f32[512,128]{0,1:T(8,128)} %copy.286) | copy-start | bytes 786436
  208.7 2.4 copy-start.21
  211.0 26.6 %copy-start.1 = (f32[512,128]{1,0:T(8,128)S(1)}, f32[512,128]{1,0:T(8,128)}, u32[]{:S(2)}) copy-start(f32[512,128]{1,0:T(8,128)} %get-tuple-element.130) | copy-start | bytes 786436
  277.4 22.2 %copy-start.2 = (pred[512,512]{1,0:T(8,128)(4,1)S(1)}, pred[512,512]{1,0:T(8,128)(4,1)}, u32[]{:S(2)}) copy-start(pred[512,512]{1,0:T(8,128)(4,1)} %fusion.31) | copy-start | bytes 786436
  277.4 22.2 %copy-start.6 = (f32[16,512]{1,0:T(8,128)S(1)}, f32[16,512]{1,0:T(8,128)}, u32[]{:S(2)}) copy-start(f32[16,512]{1,0:T(8,128)} %copy.254) | copy-start | bytes 98308
  297.1 2.6 copy-start.17
  299.0 8.7 slice-start
  299.7 8.0 slice-start.1
  299.7 8.0 copy-start.15
  299.7 8.0 copy-start.18
  307.7 6.7 copy-start.13
  307.7 6.7 copy-start.16
  314.4 6.7 copy-start.11
  314.4 6.7 copy-start.14
  321.0 6.7 copy-start.9
  321.0 6.7 copy-start.12
  327.7 7.2 copy-start.7
  327.7 7.2 copy-start.10
  334.9 6.7 copy-start.8
  711.0 24.6 %copy-start.4 = (f32[8192]{0:T(1024)S(1)}, f32[8192]{0:T(1024)}, u32[]{:S(2)}) copy-start(f32[8192]{0:T(1024)} %mul.346) | copy-start | bytes 98308
  758.8 5.7 copy-start.20
  758.8 99.6 %all-to-all-start.3 = ((bf16[8,64,8192]{2,1,0:T(8,128)(2,1)}), bf16[8,64,8192]{2,1,0:T(8,128)(2,1)}, u32[]{:S(2)}, u32[]{:S(2)}) async-start(bf16[8,64,8192]{2,1,0:T(8,128)(2,1)} %add_convert_fusion), calls=%async_computation.3 | async-start | bytes 16777216 | tf_op jit(solution)/shard_map/all_to_all | solution.py:207
  892.3 8.7 copy-start
  892.3 8.7 copy-start.5
Sparse Core Ops, SparseCore 0:
  211.1 368.1 all-gather.2
where the time goes:
time: 927 us; the launch traced here: 914 us
  waiting for transfers between devices  367 us (40%)
  local copies, waits for them, and re-layouts  261 us (28%)
  other arithmetic  150 us (16%)
  matrix products  78.3 us (8%)
  starting transfers between devices  22.7 us (2%)
  blocking collectives  19.1 us (2%)
  between operations  15.5 us (2%)
    all_gather x1, waiting for transfers between devices, entering(): everything = jax.tree.map(lambda part: lax.all_gather(part, axis), value)  175 us
    select_n x16, other arithmetic, turn(): return jax.tree.map(lambda a, b: jnp.where(reached, a, b), new, before)  95.9 us
    all_to_all x1, waiting for transfers between devices, shards(): lax.all_to_all(mixed_slots, 'dp', split_axis=0, concat_axis=0, tiled=True)  93.9 us
    all_to_all x1, waiting for transfers between devices, shards(): lax.all_to_all(pack_slots(ssm_input), 'dp', split_axis=0, concat_axis=0,...  83.9 us
    dot_general x8, matrix products, block_inner(): jnp.einsum('hqs,shp->qhp', scores, grouped_values[:, group_index], prefer...  55.1 us
    reshape x2, local copies, waits for them, and re-layouts, block_inner(): jnp.stack(inner_parts, axis=1).reshape(block_size, head_count, head_width)  49.6 us
    reshape x2, local copies, waits for them, and re-layouts, block_outer(): carried_part = jnp.einsum('qgn,ghpn->qghp', read_rows.reshape(block_size,...  49.2 us
    another operation x2, local copies, waits for them, and re-layouts, block_inner(): grouped_values = values.reshape(block_size, GROUPS, per_group, head_width)  41.9 us
  transfers between devices with their start and end apart: 5, of which 5 were waited for; matrix products, arithmetic and copies ran while one was open for 22% of the time, Pallas kernels for 0%

commit v1 on v0

v1 whole, which is shorter than its diff:
```python
import jax
import jax.numpy as jnp
from jax import lax
from jax.experimental import pallas as pl
from jax.experimental.pallas import tpu as pltpu
from jax.sharding import PartitionSpec as P

GROUPS = 8
BLOCK = 512
EPSILON = 1e-05
CHUNKS = 4
N_DP = 8
N_CTX = 16
ROWS = 256
HEADS = 16
WIDTH = 1024 // CHUNKS
STATE = 128
DOCS = 8
SLOTS = 64
MESH = pl.DeviceIdType.MESH
F32 = jnp.float32
BF16 = jnp.bfloat16


def dot(a, b, dims=((1,), (0,)), precision=None):
    return lax.dot_general(a, b, (dims, ((), ())), precision=precision, preferred_element_type=F32)


def exact(a, b, dims=((1,), (0,))):
    return dot(a, b, dims, lax.Precision.HIGHEST)


def thirds(value):
    high = value.astype(BF16).astype(F32)
    middle = (value - high).astype(BF16).astype(F32)
    low = (value - high - middle).astype(BF16).astype(F32)
    return high, middle, low


def iota(shape, dim):
    return lax.broadcasted_iota(jnp.int32, shape, dim)


def kernel(
    x_ref,
    gate_ref,
    write_ref,
    read_ref,
    packet_ref,
    rate_ref,
    skip_ref,
    gain_ref,
    out_ref,
    gate_buf,
    meta,
    writes,
    reads,
    xs,
    aux,
    aux_in,
    sums,
    sums_in,
    states,
    states_in,
    mixed,
    mixed_in,
    scores,
    scaled,
    writes_t,
    reads_m,
    factors,
    keys_row,
    keys_col,
    spread,
    local_sem,
    send_sem,
    recv_sem,
    x_send,
    x_recv,
    s_send,
    s_recv,
    h_send,
    h_recv,
    y_send,
    y_recv,
):
    me = lax.axis_index("dp")
    col = lax.axis_index("ctx")

    def remote(src, dst, send, recv, axis, peer):
        return pltpu.make_async_remote_copy(
            src_ref=src,
            dst_ref=dst,
            send_sem=send,
            recv_sem=recv,
            device_id={axis: peer},
            device_id_type=MESH,
        )

    def lanes(ref, start, width):
        return ref.at[:, pl.ds(pl.multiple_of(start, 128), width)]

    own = [
        pltpu.make_async_copy(packet_ref.at[me], meta.at[me], local_sem.at[0]),
        pltpu.make_async_copy(lanes(write_ref, me * STATE, STATE), writes.at[me], local_sem.at[1]),
        pltpu.make_async_copy(lanes(read_ref, me * STATE, STATE), reads.at[me], local_sem.at[2]),
        pltpu.make_async_copy(gate_ref, gate_buf, local_sem.at[3]),
    ]
    own_x = [
        pltpu.make_async_copy(
            lanes(x_ref, me * 1024 + c * WIDTH, WIDTH), xs.at[c, me], local_sem.at[4 + c]
        )
        for c in range(CHUNKS)
    ]
    for copy in own[:3] + own_x + own[3:]:
        copy.start()

    barrier = pltpu.get_barrier_semaphore()
    for d in range(1, N_DP):
        pl.semaphore_signal(
            barrier, inc=1, device_id={"dp": lax.rem(me + d, N_DP)}, device_id_type=MESH
        )
    for d in range(1, N_CTX):
        pl.semaphore_signal(
            barrier, inc=1, device_id={"ctx": lax.rem(col + d, N_CTX)}, device_id_type=MESH
        )
    pl.semaphore_wait(barrier, N_DP + N_CTX - 2)

    for d in range(1, N_DP):
        peer = lax.rem(me + d, N_DP)
        remote(
            packet_ref.at[peer], meta.at[me], send_sem.at[0], recv_sem.at[0], "dp", peer
        ).start()
    for d in range(1, N_DP):
        peer = lax.rem(me + d, N_DP)
        remote(
            lanes(write_ref, peer * STATE, STATE),
            writes.at[me],
            send_sem.at[1],
            recv_sem.at[1],
            "dp",
            peer,
        ).start()
        remote(
            lanes(read_ref, peer * STATE, STATE),
            reads.at[me],
            send_sem.at[2],
            recv_sem.at[2],
            "dp",
            peer,
        ).start()
    for c in range(CHUNKS):
        for d in range(1, N_DP):
            peer = lax.rem(me + d, N_DP)
            remote(
                lanes(x_ref, peer * 1024 + c * WIDTH, WIDTH),
                xs.at[c, me],
                x_send.at[c],
                x_recv.at[c],
                "dp",
                peer,
            ).start()

    row = iota((128, WIDTH), 0)
    for c in range(CHUNKS):
        head = c * (HEADS // CHUNKS) + iota((128, WIDTH), 1) // 64
        named = lax.rem(row, HEADS) == head
        spread[0, c] = jnp.where(named & (row < 48), 1.0, 0.0).astype(BF16)
        spread[1, c] = jnp.where(named & (row >= 48) & (row < 96), 1.0, 0.0).astype(BF16)

    def arrived(ref, count, sem):
        part = ref.at[pl.ds(0, count)]
        pltpu.make_async_copy(part, part, sem).wait()

    own[0].wait()
    arrived(meta, N_DP - 1, recv_sem.at[0])
    first_slot = (col * BLOCK).astype(F32)

    owners = meta[:, 16, :]
    lengths = meta[:, 17, :]
    starts = []
    total = jnp.zeros((N_DP, 1), F32)
    for d in range(DOCS):
        starts.append(total)
        total = total + lengths[:, d : d + 1]
    sequence = iota((N_DP, 1), 0).astype(F32)
    table = jnp.where(
        owners[:, None, :] == iota((N_DP, N_DP, ROWS), 1).astype(F32), 1.0, 0.0
    )
    earlier = jnp.where(iota((ROWS, ROWS), 0) < iota((ROWS, ROWS), 1), 1.0, 0.0)
    counts = dot(table.reshape(N_DP * N_DP, ROWS).astype(BF16), earlier.astype(BF16))
    rank = jnp.sum(table * counts.reshape(N_DP, N_DP, ROWS), axis=1)
    slot = first_slot + (iota((N_DP, ROWS), 0) * SLOTS).astype(F32) + rank
    segment = jnp.zeros((N_DP, N_DP, ROWS), F32)
    before = jnp.zeros((N_DP, 1), F32)
    end = jnp.zeros((N_DP, 1), F32)
    for d in range(DOCS):
        segment = segment + jnp.where(slot[:, None, :] >= starts[d][None], 1.0, 0.0)
        before = before + jnp.where(first_slot - 1.0 >= starts[d], 1.0, 0.0)
        end = end + jnp.where(first_slot + (BLOCK - 1.0) >= starts[d], 1.0, 0.0)
    key = owners * 16.0 + jnp.sum(table * segment, axis=1)
    key_before = sequence * 16.0 + before
    key_end = sequence * 16.0 + end
    same_document = jnp.where(key_before == key_end, 1.0, 0.0)
    keys_row[...] = key
    key_t = key.T
    owner_t = owners.T

    rate_row = rate_ref[pl.ds(me, 1), :]
    rate = jnp.sum(
        jnp.where(iota((HEADS, HEADS), 0) == iota((HEADS, HEADS), 1), rate_row, 0.0),
        axis=1,
        keepdims=True,
    )
    not_later = iota((ROWS, ROWS), 0) <= iota((ROWS, ROWS), 1)
    sofar = jnp.zeros((HEADS, N_DP), F32)
    whole_t = jnp.zeros((N_DP, HEADS), F32)
    running = []
    for i in range(N_DP):
        keys_col[i] = jnp.broadcast_to(key_t[:, i : i + 1], (ROWS, 128))
        step = meta[i, 0:HEADS, :].astype(BF16)
        owned = table[i]
        same = jnp.where((owner_t[:, i : i + 1] == owners[i : i + 1, :]) & not_later, 1.0, 0.0)
        running.append(dot(step, same.astype(BF16)) + exact(sofar, owned))
        sofar = sofar + dot(step, owned.astype(BF16), ((1,), (1,)))
        whole_t = whole_t + dot(owned.astype(BF16), step, ((1,), (1,)))
    middle = -0.5 * rate * sofar
    for i in range(N_DP):
        exponent = -rate * running[i] - exact(middle, table[i])
        rising = thirds(jnp.exp(-exponent) * meta[i, 0:HEADS, :])
        falling = thirds(jnp.exp(exponent))
        stack = jnp.concatenate(falling + rising + (jnp.zeros((32, ROWS), F32),), axis=0)
        factors[i] = stack.T.astype(BF16)
    middle_t = -0.5 * whole_t * rate_row
    half_decay = thirds(jnp.exp(middle_t))
    full_decay = thirds(jnp.exp(2.0 * middle_t) * same_document)
    for c in range(CHUNKS):
        heads = spread[0, c, 0:HEADS, :]
        half = sum(dot(part.astype(BF16), heads) for part in half_decay)
        full = sum(dot(part.astype(BF16), heads) for part in full_decay)
        for k in range(N_DP):
            aux[k, 0:1, c * WIDTH : (c + 1) * WIDTH] = full[k : k + 1, :]
            aux[k, 1:2, c * WIDTH : (c + 1) * WIDTH] = half[k : k + 1, :]
    for k in range(N_DP):
        aux[k, 2:8, :] = jnp.zeros((6, 1024), F32)
    for d in range(1, N_CTX):
        peer = lax.rem(col + d, N_CTX)
        remote(
            aux.at[peer // 2], aux_in.at[col], send_sem.at[3], recv_sem.at[3], "ctx", peer
        ).start()
    aux_in[col] = aux[col // 2]

    own[1].wait()
    arrived(writes, N_DP - 1, recv_sem.at[1])
    for i in range(N_DP):
        flipped = writes[i].astype(F32).T
        for k in range(N_DP):
            kept = keys_row[i : i + 1, :] == key_end[k : k + 1, :]
            writes_t[k, :, i * ROWS : (i + 1) * ROWS] = jnp.where(kept, flipped, 0.0).astype(BF16)
    own[2].wait()
    arrived(reads, N_DP - 1, recv_sem.at[2])

    for i in range(N_DP):
        block = reads[i].astype(F32)
        for k in range(N_DP):
            kept = keys_col[i] == key_before[k : k + 1, :]
            reads_m[i, :, k * STATE : (k + 1) * STATE] = jnp.where(kept, block, 0.0).astype(BF16)

    ordered = iota((ROWS, ROWS), 0) >= iota((ROWS, ROWS), 1)

    def score_rows(i, carry):
        key_q = keys_col[i][:, 0:1]
        block = reads[i]

        def score(j, carry):
            raw = dot(block, writes[j], ((1,), (1,)))
            kept = (key_q == keys_row[pl.ds(j, 1), :]) & (ordered | (j < i))
            scores[i, :, pl.ds(pl.multiple_of(j * ROWS, ROWS), ROWS)] = jnp.where(
                kept, raw, 0.0
            ).astype(BF16)
            return carry

        return lax.fori_loop(0, i + 1, score, carry)

    lax.fori_loop(0, N_DP, score_rows, 0)

    def summarize(c):
        pltpu.make_async_copy(xs.at[0, 0], xs.at[0, 0], local_sem.at[4 + c]).wait()
        arrived(xs.at[c], N_DP - 1, x_recv.at[c])

        def scale(i, carry):
            factor = dot(factors[i], spread[1, c])
            scaled[c, pl.ds(pl.multiple_of(i * ROWS, ROWS), ROWS), :] = (
                xs[c, i].astype(F32) * factor
            ).astype(BF16)
            return carry

        lax.fori_loop(0, N_DP, scale, 0)

        def collect(k, carry):
            part = dot(writes_t[k], scaled[c])
            half = aux[k, 1:2, pl.ds(pl.multiple_of(c * WIDTH, WIDTH), WIDTH)]
            part = (part * half).astype(BF16)
            sums[c, 2 * k] = part[0:64]
            sums[c, 2 * k + 1] = part[64:128]
            return carry

        lax.fori_loop(0, N_DP, collect, 0)
        for d in range(1, N_CTX):
            peer = lax.rem(col + d, N_CTX)
            remote(
                sums.at[c, peer], sums_in.at[c, col], s_send.at[c], s_recv.at[c], "ctx", peer
            ).start()
        sums_in[c, col] = sums[c, col]

    def carry_on(c):
        @pl.when(c == 0)
        def _():
            arrived(aux_in, N_CTX - 1, recv_sem.at[3])

        arrived(sums_in.at[c], N_CTX - 1, s_recv.at[c])
        window = pl.ds(pl.multiple_of(c * WIDTH, WIDTH), WIDTH)

        def advance(j, held):
            states[c, j] = (held * aux_in[j, 1:2, window]).astype(BF16)
            return held * aux_in[j, 0:1, window] + sums_in[c, j].astype(F32)

        lax.fori_loop(0, N_CTX, advance, jnp.zeros((64, WIDTH), F32))
        for d in range(1, N_CTX):
            peer = lax.rem(col + d, N_CTX)
            remote(
                states.at[c, peer], states_in.at[c, col], h_send.at[c], h_recv.at[c], "ctx", peer
            ).start()
        states_in[c, col] = states[c, col]

    def mix(c):
        arrived(states_in.at[c], N_CTX - 1, h_recv.at[c])
        carried = states_in[c].reshape(N_DP * STATE, WIDTH)
        skip = skip_ref[pl.ds(me, 1), pl.ds(pl.multiple_of(c * WIDTH, WIDTH), WIDTH)]
        for i in range(N_DP):
            reach = (i + 1) * ROWS
            both = dot(scores[i, :, 0:reach], scaled[c, 0:reach, :]) + dot(reads_m[i], carried)
            factor = dot(factors[i], spread[0, c])
            mixed[c, i] = (both * factor + skip * xs[c, i].astype(F32)).astype(BF16)

            @pl.when(me != i)
            def _():
                remote(
                    mixed.at[c, i], mixed_in.at[c, me], y_send.at[c], y_recv.at[c], "dp", i
                ).start()

        mixed_in[c, me] = mixed[c, me]

    def step(s, carry):
        @pl.when(s < CHUNKS)
        def _():
            summarize(s)

        @pl.when(s > 0)
        def _():
            mix(s - 1)

        @pl.when(s < CHUNKS)
        def _():
            carry_on(s)

        return carry

    lax.fori_loop(0, CHUNKS + 1, step, 0)

    own[3].wait()
    for c in range(CHUNKS):
        arrived(mixed_in.at[c], N_DP - 1, y_recv.at[c])

    def finish(g, carry):
        gated = []
        squares = jnp.zeros((ROWS, 1), F32)
        for c in range(CHUNKS):
            place = pl.ds(pl.multiple_of(g * 1024 + c * WIDTH, WIDTH), WIDTH)
            gate = gate_buf[:, place].astype(F32)
            part = mixed_in[c, g].astype(F32) * (gate / (1.0 + jnp.exp(-gate)))
            squares = squares + jnp.sum(part * part, axis=1, keepdims=True)
            gated.append(part)
        inverse = lax.rsqrt(squares * (1.0 / 1024.0) + EPSILON)
        for c in range(CHUNKS):
            place = pl.ds(pl.multiple_of(g * 1024 + c * WIDTH, WIDTH), WIDTH)
            out_ref[:, place] = (gated[c] * inverse * gain_ref[:, place]).astype(BF16)
        return carry

    lax.fori_loop(0, GROUPS, finish, 0)

    arrived(meta, N_DP - 1, send_sem.at[0])
    arrived(writes, N_DP - 1, send_sem.at[1])
    arrived(reads, N_DP - 1, send_sem.at[2])
    arrived(aux_in, N_CTX - 1, send_sem.at[3])
    for c in range(CHUNKS):
        arrived(xs.at[c], N_DP - 1, x_send.at[c])
        arrived(sums_in.at[c], N_CTX - 1, s_send.at[c])
        arrived(states_in.at[c], N_CTX - 1, h_send.at[c])
        arrived(mixed_in.at[c], N_DP - 1, y_send.at[c])


def shards(
    ssm_input,
    gate_input,
    write_basis,
    read_basis,
    step_size,
    decay_rate,
    skip_weight,
    norm_gain,
    row_owner,
    document_lengths,
):
    steps = step_size.astype(F32).T.reshape(GROUPS, HEADS, ROWS)
    owners = row_owner.astype(F32).reshape(1, 1, ROWS)
    lengths = jnp.pad(document_lengths.astype(F32), ((0, 0), (0, ROWS - DOCS))).reshape(1, 1, ROWS)
    packet = jnp.concatenate(
        [
            steps,
            jnp.broadcast_to(owners, (GROUPS, 1, ROWS)),
            jnp.broadcast_to(lengths, (GROUPS, 1, ROWS)),
            jnp.zeros((GROUPS, 6, ROWS), F32),
        ],
        axis=1,
    )
    rates = decay_rate.reshape(GROUPS, HEADS)
    skips = jnp.repeat(skip_weight, 64).reshape(GROUPS, 1024)
    gains = norm_gain.reshape(1, -1)
    hbm = pl.BlockSpec(memory_space=pl.ANY)
    vmem = pl.BlockSpec(memory_space=pltpu.VMEM)
    dma = pltpu.SemaphoreType.DMA
    return pl.pallas_call(
        kernel,
        out_shape=jax.ShapeDtypeStruct((ROWS, GROUPS * 1024), BF16),
        in_specs=[hbm, hbm, hbm, hbm, hbm, vmem, vmem, vmem],
        out_specs=vmem,
        scratch_shapes=[
            pltpu.VMEM((ROWS, GROUPS * 1024), BF16),
            pltpu.VMEM((N_DP, 24, ROWS), F32),
            pltpu.VMEM((N_DP, ROWS, STATE), BF16),
            pltpu.VMEM((N_DP, ROWS, STATE), BF16),
            pltpu.VMEM((CHUNKS, N_DP, ROWS, WIDTH), BF16),
            pltpu.VMEM((N_DP, 8, 1024), F32),
            pltpu.VMEM((N_CTX, 8, 1024), F32),
            pltpu.VMEM((CHUNKS, N_CTX, 64, WIDTH), BF16),
            pltpu.VMEM((CHUNKS, N_CTX, 64, WIDTH), BF16),
            pltpu.VMEM((CHUNKS, N_CTX, 64, WIDTH), BF16),
            pltpu.VMEM((CHUNKS, N_CTX, 64, WIDTH), BF16),
            pltpu.VMEM((CHUNKS, N_DP, ROWS, WIDTH), BF16),
            pltpu.VMEM((CHUNKS, N_DP, ROWS, WIDTH), BF16),
            pltpu.VMEM((N_DP, ROWS, N_DP * ROWS), BF16),
            pltpu.VMEM((CHUNKS, N_DP * ROWS, WIDTH), BF16),
            pltpu.VMEM((N_DP, STATE, N_DP * ROWS), BF16),
            pltpu.VMEM((N_DP, ROWS, N_DP * STATE), BF16),
            pltpu.VMEM((N_DP, ROWS, 128), BF16),
            pltpu.VMEM((N_DP, ROWS), F32),
            pltpu.VMEM((N_DP, ROWS, 128), F32),
            pltpu.VMEM((2, CHUNKS, 128, WIDTH), BF16),
            dma((4 + CHUNKS,)),
            dma((4,)),
            dma((4,)),
            dma((CHUNKS,)),
            dma((CHUNKS,)),
            dma((CHUNKS,)),
            dma((CHUNKS,)),
            dma((CHUNKS,)),
            dma((CHUNKS,)),
            dma((CHUNKS,)),
            dma((CHUNKS,)),
        ],
        compiler_params=pltpu.CompilerParams(
            collective_id=0, has_side_effects=True, vmem_limit_bytes=60 * 2**20
        ),
        cost_estimate=pl.CostEstimate(
            flops=14 * 10**9, bytes_accessed=16 * 2**20, transcendentals=4 * 10**6
        ),
    )(ssm_input, gate_input, write_basis, read_basis, packet, rates, skips, gains)


def solution(mesh):
    placed = (
        P(("dp", "ctx"), None),
        P(("dp", "ctx"), None),
        P(("dp", "ctx"), None),
        P(("dp", "ctx"), None),
        P(("dp", "ctx"), None),
        P(),
        P(),
        P(),
        P(("dp", "ctx"), None),
        P("dp", None),
    )
    return jax.shard_map(
        shards, mesh=mesh, in_specs=placed, out_specs=P(("dp", "ctx"), None), check_vma=False
    )
```

time: 927 us -> 134 us (0.14); the launches traced: 914 us -> 132 us
  waiting for transfers between devices: 367 us -> 0 us
  local copies, waits for them, and re-layouts: 261 us -> 7.65 us
  other arithmetic: 150 us -> 2.95 us
  Pallas kernels: 0 us -> 122 us
  matrix products: 78.3 us -> 0 us
  starting transfers between devices: 22.7 us -> 0 us
  blocking collectives: 19.1 us -> 0 us
  between operations: 15.5 us -> 0.04 us
    all_to_all x4 -> x0, waiting for transfers between devices: 193 us -> none  [the longest x1 93.9 us: shards(): lax.all_to_all(mixed_slots, 'dp', split_axis=0, concat_axis=0, tiled=True)]
    all_gather x1 -> x0, waiting for transfers between devices: 175 us -> none  [entering(): everything = jax.tree.map(lambda part: lax.all_gather(part, axis), value)]
    pallas_call x0 -> x1, Pallas kernels: none -> 122 us  [shards(): pl.pallas_call(kernel, out_shape=jax.ShapeDtypeStruct((ROWS, GROUPS * 102...]
    reshape x4 -> x2, local copies, waits for them, and re-layouts: 98.9 us -> 1.42 us  [the longest x1 1.32 us: shards(): rates = decay_rate.reshape(GROUPS, HEADS)]
    select_n x17 -> x0, other arithmetic: 96.6 us -> none  [the longest x16 95.9 us: turn(): return jax.tree.map(lambda a, b: jnp.where(reached, a, b), new, before)]
    dot_general x18 -> x0, matrix products: 78.3 us -> none  [the longest x8 55.1 us: block_inner(): jnp.einsum('hqs,shp->qhp', scores, grouped_values[:, group_index], prefer...]
    mul x22 -> x0, local copies, waits for them, and re-layouts: 42.2 us -> none  [the longest x2 39.9 us: block_outer(): return carried_part * factor[:, :, None] + direct]
    another operation x6 -> x0, local copies, waits for them, and re-layouts: 42 us -> none  [the longest x2 41.9 us: block_inner(): grouped_values = values.reshape(block_size, GROUPS, per_group, head_width)]
  transfers between devices with their start and end apart: 5 -> 0, of which waited for: 5 -> 0; matrix products, arithmetic and copies ran while one was open for 22% -> 0% of each run, Pallas kernels for 0% -> 0%
where the time goes in v1:
time: 134 us; the launch traced here: 132 us
  Pallas kernels  122 us (91%)
  local copies, waits for them, and re-layouts  7.65 us (6%)
  other arithmetic  2.95 us (2%)
    pallas_call x1, Pallas kernels, shards(): pl.pallas_call(kernel, out_shape=jax.ShapeDtypeStruct((ROWS, GROUPS * 102...  122 us
    unnamed x1, local copies, waits for them, and re-layouts  4.64 us

profile of v1, /device:TPU:1, one launch (start us, length us, event | category | flops | bytes accessed | tf_op | source)
XLA Modules:
  0.0 132.3 jit_solution(14663630269762775834)
XLA Ops:
  0.0 0.7 convert_element_type.10
  0.7 0.1 pad.8.clone
  0.7 0.7 convert_element_type.9
  1.4 1.3 reshape.24.rate_ref
  2.8 0.7 broadcast_in_dim.29
  3.5 0.1 broadcast_in_dim.30
  3.6 0.7 broadcast_in_dim.31.skip_ref
  4.3 0.8 convert_bitcast_fusion
  5.1 0.1 copy.11
  5.2 0.8 maximum_maximum_fusion.packet_ref
  6.0 121.7 %shard_map.100 = bf16[256,8192]{1,0:T(8,128)(2,1)} custom-call(bf16[256,8192]{1,0:T(8,128)(2,1)} %x_ref.1, bf16[256,8192]{1,0:T(8,128)(2,1)} %gate_ref.1, bf16[256,1024]{1,0:T(8,128)(2,1)} %write_ref.1, bf16[256,1024]{1,0:T(8,128)(2,1)} %read_ref.1, f32[8,24,256]{2,1,0:T(8,128)} %maximum_maximum_fusion.packet_ref, f32[8,16]{1,0:T(8,128)} %reshape.24.rate_ref, ...), custom_call_target="tpu_custom_call" | custom-call | flops 14000000000 | bytes 16777216 | tf_op jit(solution)/shard_map/pallas_call | solution.py:433
  127.7 4.6 %copy.13 = bf16[256,8192]{1,0:T(8,128)(2,1)} copy(bf16[256,8192]{1,0:T(8,128)(2,1)} %shard_map.100) | data formatting | bytes 8388608
  (4 shorter events, 0.0 us)

commit v2 on v1

--- a/solution.py
+++ b/solution.py
@@ -43,15 +43,21 @@
 
 def kernel(
     x_ref,
-    gate_ref,
     write_ref,
     read_ref,
-    packet_ref,
+    step_ref,
+    owner_hbm,
+    length_hbm,
+    rate_hbm,
+    skip_hbm,
+    out_ref,
+    owner_ref,
+    length_ref,
     rate_ref,
     skip_ref,
-    gain_ref,
-    out_ref,
-    gate_buf,
+    steps,
+    packet,
+    skips,
     meta,
     writes,
     reads,
@@ -63,7 +69,6 @@
     states,
     states_in,
     mixed,
-    mixed_in,
     scores,
     scaled,
     writes_t,
@@ -72,6 +77,7 @@
     keys_row,
     keys_col,
     spread,
+    small_sem,
     local_sem,
     send_sem,
     recv_sem,
@@ -100,20 +106,8 @@
     def lanes(ref, start, width):
         return ref.at[:, pl.ds(pl.multiple_of(start, 128), width)]
 
-    own = [
-        pltpu.make_async_copy(packet_ref.at[me], meta.at[me], local_sem.at[0]),
-        pltpu.make_async_copy(lanes(write_ref, me * STATE, STATE), writes.at[me], local_sem.at[1]),
-        pltpu.make_async_copy(lanes(read_ref, me * STATE, STATE), reads.at[me], local_sem.at[2]),
-        pltpu.make_async_copy(gate_ref, gate_buf, local_sem.at[3]),
-    ]
-    own_x = [
-        pltpu.make_async_copy(
-            lanes(x_ref, me * 1024 + c * WIDTH, WIDTH), xs.at[c, me], local_sem.at[4 + c]
-        )
-        for c in range(CHUNKS)
-    ]
-    for copy in own[:3] + own_x + own[3:]:
-        copy.start()
+    def piece(ref, owner, c):
+        return lanes(ref, owner * 1024 + c * WIDTH, WIDTH)
 
     barrier = pltpu.get_barrier_semaphore()
     for d in range(1, N_DP):
@@ -124,13 +118,26 @@
         pl.semaphore_signal(
             barrier, inc=1, device_id={"ctx": lax.rem(col + d, N_CTX)}, device_id_type=MESH
         )
+
+    own = [
+        pltpu.make_async_copy(step_ref, steps, local_sem.at[0]),
+        pltpu.make_async_copy(lanes(write_ref, me * STATE, STATE), writes.at[me], local_sem.at[1]),
+        pltpu.make_async_copy(lanes(read_ref, me * STATE, STATE), reads.at[me], local_sem.at[2]),
+    ]
+    own_x = [
+        pltpu.make_async_copy(piece(x_ref, me, c), xs.at[c, me], local_sem.at[4 + c])
+        for c in range(CHUNKS)
+    ]
+    small = [
+        pltpu.make_async_copy(owner_hbm, owner_ref, small_sem.at[0]),
+        pltpu.make_async_copy(length_hbm, length_ref, small_sem.at[1]),
+        pltpu.make_async_copy(rate_hbm, rate_ref, small_sem.at[2]),
+        pltpu.make_async_copy(skip_hbm, skip_ref, small_sem.at[3]),
+    ]
+    for copy in own[:1] + small + own[1:] + own_x:
+        copy.start()
     pl.semaphore_wait(barrier, N_DP + N_CTX - 2)
 
-    for d in range(1, N_DP):
-        peer = lax.rem(me + d, N_DP)
-        remote(
-            packet_ref.at[peer], meta.at[me], send_sem.at[0], recv_sem.at[0], "dp", peer
-        ).start()
     for d in range(1, N_DP):
         peer = lax.rem(me + d, N_DP)
         remote(
@@ -149,16 +156,32 @@
             "dp",
             peer,
         ).start()
+
+    own[0].wait()
+    for copy in small:
+        copy.wait()
+    packet[:, 0:HEADS, :] = steps[...].astype(F32).T.reshape(GROUPS, HEADS, ROWS).astype(BF16)
+    owner_row = owner_ref[...].astype(F32)
+    line = iota((16, ROWS), 0)
+    lane = iota((16, ROWS), 1)
+    extra = jnp.where(line == 0, owner_row, 0.0)
+    for d in range(DOCS):
+        length = length_ref[0:1, d : d + 1]
+        extra = jnp.where((line == 1) & (lane == d), (length // 64).astype(F32), extra)
+        extra = jnp.where((line == 2) & (lane == d), (length % 64).astype(F32), extra)
+    for k in range(GROUPS):
+        packet[k, 16:32, :] = extra.astype(BF16)
+    for d in range(1, N_DP):
+        peer = lax.rem(me + d, N_DP)
+        remote(
+            packet.at[peer], meta.at[me], send_sem.at[0], recv_sem.at[0], "dp", peer
+        ).start()
+    meta[me] = packet[me]
     for c in range(CHUNKS):
         for d in range(1, N_DP):
             peer = lax.rem(me + d, N_DP)
             remote(
-                lanes(x_ref, peer * 1024 + c * WIDTH, WIDTH),
-                xs.at[c, me],
-                x_send.at[c],
-                x_recv.at[c],
-                "dp",
-                peer,
+                piece(x_ref, peer, c), xs.at[c, me], x_send.at[c], x_recv.at[c], "dp", peer
             ).start()
 
     row = iota((128, WIDTH), 0)
@@ -167,17 +190,19 @@
         named = lax.rem(row, HEADS) == head
         spread[0, c] = jnp.where(named & (row < 48), 1.0, 0.0).astype(BF16)
         spread[1, c] = jnp.where(named & (row >= 48) & (row < 96), 1.0, 0.0).astype(BF16)
+        mine = jnp.where(row == me * HEADS + head, 1.0, 0.0)
+        skips[c] = exact(jnp.broadcast_to(skip_ref[...], (8, 128)), mine)
 
     def arrived(ref, count, sem):
         part = ref.at[pl.ds(0, count)]
         pltpu.make_async_copy(part, part, sem).wait()
 
-    own[0].wait()
     arrived(meta, N_DP - 1, recv_sem.at[0])
     first_slot = (col * BLOCK).astype(F32)
 
-    owners = meta[:, 16, :]
-    lengths = meta[:, 17, :]
+    extras = meta[:, 16:32, :].astype(F32)
+    owners = extras[:, 0, :]
+    lengths = extras[:, 1, :] * 64.0 + extras[:, 2, :]
     starts = []
     total = jnp.zeros((N_DP, 1), F32)
     for d in range(DOCS):
@@ -206,10 +231,16 @@
     key_t = key.T
     owner_t = owners.T
 
-    rate_row = rate_ref[pl.ds(me, 1), :]
     rate = jnp.sum(
-        jnp.where(iota((HEADS, HEADS), 0) == iota((HEADS, HEADS), 1), rate_row, 0.0),
+        jnp.where(
+            iota((HEADS, 128), 1) == iota((HEADS, 128), 0) + me * HEADS, rate_ref[...], 0.0
+        ),
         axis=1,
+        keepdims=True,
+    )
+    rate_row = jnp.sum(
+        jnp.where(iota((HEADS, HEADS), 0) == iota((HEADS, HEADS), 1), rate, 0.0),
+        axis=0,
         keepdims=True,
     )
     not_later = iota((ROWS, ROWS), 0) <= iota((ROWS, ROWS), 1)
@@ -218,7 +249,7 @@
     running = []
     for i in range(N_DP):
         keys_col[i] = jnp.broadcast_to(key_t[:, i : i + 1], (ROWS, 128))
-        step = meta[i, 0:HEADS, :].astype(BF16)
+        step = meta[i, 0:HEADS, :]
         owned = table[i]
         same = jnp.where((owner_t[:, i : i + 1] == owners[i : i + 1, :]) & not_later, 1.0, 0.0)
         running.append(dot(step, same.astype(BF16)) + exact(sofar, owned))
@@ -227,7 +258,7 @@
     middle = -0.5 * rate * sofar
     for i in range(N_DP):
         exponent = -rate * running[i] - exact(middle, table[i])
-        rising = thirds(jnp.exp(-exponent) * meta[i, 0:HEADS, :])
+        rising = thirds(jnp.exp(-exponent) * meta[i, 0:HEADS, :].astype(F32))
         falling = thirds(jnp.exp(exponent))
         stack = jnp.concatenate(falling + rising + (jnp.zeros((32, ROWS), F32),), axis=0)
         factors[i] = stack.T.astype(BF16)
@@ -298,19 +329,23 @@
         lax.fori_loop(0, N_DP, scale, 0)
 
         def collect(k, carry):
+            k = lax.rem(k + col // 2, N_DP)
             part = dot(writes_t[k], scaled[c])
             half = aux[k, 1:2, pl.ds(pl.multiple_of(c * WIDTH, WIDTH), WIDTH)]
             part = (part * half).astype(BF16)
-            sums[c, 2 * k] = part[0:64]
-            sums[c, 2 * k + 1] = part[64:128]
+            for side in range(2):
+                peer = 2 * k + side
+                sums[c, peer] = part[64 * side : 64 * side + 64]
+
+                @pl.when(peer != col)
+                def _():
+                    remote(
+                        sums.at[c, peer], sums_in.at[c, col], s_send.at[c], s_recv.at[c], "ctx", peer
+                    ).start()
+
             return carry
 
         lax.fori_loop(0, N_DP, collect, 0)
-        for d in range(1, N_CTX):
-            peer = lax.rem(col + d, N_CTX)
-            remote(
-                sums.at[c, peer], sums_in.at[c, col], s_send.at[c], s_recv.at[c], "ctx", peer
-            ).start()
         sums_in[c, col] = sums[c, col]
 
     def carry_on(c):
@@ -333,10 +368,16 @@
             ).start()
         states_in[c, col] = states[c, col]
 
+    def hand_back(c, peer):
+        remote(
+            mixed.at[c, peer], piece(out_ref, me, c), y_send.at[c], y_recv.at[c], "dp", peer
+        ).start()
+
     def mix(c):
         arrived(states_in.at[c], N_CTX - 1, h_recv.at[c])
+
         carried = states_in[c].reshape(N_DP * STATE, WIDTH)
-        skip = skip_ref[pl.ds(me, 1), pl.ds(pl.multiple_of(c * WIDTH, WIDTH), WIDTH)]
+        skip = skips[c, 0:1, :]
         for i in range(N_DP):
             reach = (i + 1) * ROWS
             both = dot(scores[i, :, 0:reach], scaled[c, 0:reach, :]) + dot(reads_m[i], carried)
@@ -345,49 +386,30 @@
 
             @pl.when(me != i)
             def _():
-                remote(
-                    mixed.at[c, i], mixed_in.at[c, me], y_send.at[c], y_recv.at[c], "dp", i
-                ).start()
-
-        mixed_in[c, me] = mixed[c, me]
+                hand_back(c, i)
+
+        pltpu.make_async_copy(mixed.at[c, me], piece(out_ref, me, c), local_sem.at[3]).start()
 
     def step(s, carry):
         @pl.when(s < CHUNKS)
         def _():
             summarize(s)
 
-        @pl.when(s > 0)
+        @pl.when((s > 0) & (s < CHUNKS + 1))
         def _():
-            mix(s - 1)
-
-        @pl.when(s < CHUNKS)
+            carry_on(s - 1)
+
+        @pl.when(s > 1)
         def _():
-            carry_on(s)
+            mix(s - 2)
 
         return carry
 
-    lax.fori_loop(0, CHUNKS + 1, step, 0)
-
-    own[3].wait()
+    lax.fori_loop(0, CHUNKS + 2, step, 0)
+
+    arrived(mixed.at[0], CHUNKS, local_sem.at[3])
     for c in range(CHUNKS):
-        arrived(mixed_in.at[c], N_DP - 1, y_recv.at[c])
-
-    def finish(g, carry):
-        gated = []
-        squares = jnp.zeros((ROWS, 1), F32)
-        for c in range(CHUNKS):
-            place = pl.ds(pl.multiple_of(g * 1024 + c * WIDTH, WIDTH), WIDTH)
-            gate = gate_buf[:, place].astype(F32)
-            part = mixed_in[c, g].astype(F32) * (gate / (1.0 + jnp.exp(-gate)))
-            squares = squares + jnp.sum(part * part, axis=1, keepdims=True)
-            gated.append(part)
-        inverse = lax.rsqrt(squares * (1.0 / 1024.0) + EPSILON)
-        for c in range(CHUNKS):
-            place = pl.ds(pl.multiple_of(g * 1024 + c * WIDTH, WIDTH), WIDTH)
-            out_ref[:, place] = (gated[c] * inverse * gain_ref[:, place]).astype(BF16)
-        return carry
-
-    lax.fori_loop(0, GROUPS, finish, 0)
+        arrived(mixed.at[c], N_DP - 1, y_recv.at[c])
 
     arrived(meta, N_DP - 1, send_sem.at[0])
     arrived(writes, N_DP - 1, send_sem.at[1])
@@ -397,7 +419,31 @@
         arrived(xs.at[c], N_DP - 1, x_send.at[c])
         arrived(sums_in.at[c], N_CTX - 1, s_send.at[c])
         arrived(states_in.at[c], N_CTX - 1, h_send.at[c])
-        arrived(mixed_in.at[c], N_DP - 1, y_send.at[c])
+        arrived(mixed.at[c], N_DP - 1, y_send.at[c])
+
+
+def finish(mixed_hbm, gate_hbm, gain_ref, out_ref, mixed, gates, done, load_sem, done_sem):
+    def part(ref, g):
+        return ref.at[:, pl.ds(pl.multiple_of(g * 1024, 1024), 1024)]
+
+    for g in range(GROUPS):
+        pltpu.make_async_copy(part(gate_hbm, g), gates.at[g], load_sem.at[0, g]).start()
+        pltpu.make_async_copy(part(mixed_hbm, g), mixed.at[g], load_sem.at[1, g]).start()
+
+    def group(g, carry):
+        pltpu.make_async_copy(part(gate_hbm, g), gates.at[g], load_sem.at[0, g]).wait()
+        pltpu.make_async_copy(part(mixed_hbm, g), mixed.at[g], load_sem.at[1, g]).wait()
+        gate = gates[g].astype(F32)
+        gated = mixed[g].astype(F32) * (gate / (1.0 + jnp.exp(-gate)))
+        inverse = lax.rsqrt(jnp.mean(gated * gated, axis=1, keepdims=True) + EPSILON)
+        gain = gain_ref[:, pl.ds(pl.multiple_of(g * 1024, 1024), 1024)]
+        done[g] = (gated * inverse * gain).astype(BF16)
+        pltpu.make_async_copy(done.at[g], part(out_ref, g), done_sem.at[g]).start()
+        return carry
+
+    lax.fori_loop(0, GROUPS, group, 0)
+    for g in range(GROUPS):
+        pltpu.make_async_copy(done.at[g], part(out_ref, g), done_sem.at[g]).wait()
 
 
 def shards(
@@ -412,32 +458,24 @@
     row_owner,
     document_lengths,
 ):
-    steps = step_size.astype(F32).T.reshape(GROUPS, HEADS, ROWS)
-    owners = row_owner.astype(F32).reshape(1, 1, ROWS)
-    lengths = jnp.pad(document_lengths.astype(F32), ((0, 0), (0, ROWS - DOCS))).reshape(1, 1, ROWS)
-    packet = jnp.concatenate(
-        [
-            steps,
-            jnp.broadcast_to(owners, (GROUPS, 1, ROWS)),
-            jnp.broadcast_to(lengths, (GROUPS, 1, ROWS)),
-            jnp.zeros((GROUPS, 6, ROWS), F32),
-        ],
-        axis=1,
-    )
-    rates = decay_rate.reshape(GROUPS, HEADS)
-    skips = jnp.repeat(skip_weight, 64).reshape(GROUPS, 1024)
-    gains = norm_gain.reshape(1, -1)
-    hbm = pl.BlockSpec(memory_space=pl.ANY)
+    hbm = pl.BlockSpec(memory_space=pltpu.HBM)
+    anywhere = pl.BlockSpec(memory_space=pl.ANY)
     vmem = pl.BlockSpec(memory_space=pltpu.VMEM)
     dma = pltpu.SemaphoreType.DMA
-    return pl.pallas_call(
+    mixed = pl.pallas_call(
         kernel,
         out_shape=jax.ShapeDtypeStruct((ROWS, GROUPS * 1024), BF16),
-        in_specs=[hbm, hbm, hbm, hbm, hbm, vmem, vmem, vmem],
-        out_specs=vmem,
+        in_specs=[hbm] * 8,
+        out_specs=anywhere,
         scratch_shapes=[
-            pltpu.VMEM((ROWS, GROUPS * 1024), BF16),
-            pltpu.VMEM((N_DP, 24, ROWS), F32),
+            pltpu.VMEM((1, ROWS), jnp.int32),
+            pltpu.VMEM((1, DOCS), jnp.int32),
+            pltpu.VMEM((1, 128), F32),
+            pltpu.VMEM((1, 128), F32),
+            pltpu.VMEM((ROWS, 128), BF16),
+            pltpu.VMEM((N_DP, 32, ROWS), BF16),
+            pltpu.VMEM((CHUNKS, 8, WIDTH), F32),
+            pltpu.VMEM((N_DP, 32, ROWS), BF16),
             pltpu.VMEM((N_DP, ROWS, STATE), BF16),
             pltpu.VMEM((N_DP, ROWS, STATE), BF16),
             pltpu.VMEM((CHUNKS, N_DP, ROWS, WIDTH), BF16),
@@ -448,7 +486,6 @@
             pltpu.VMEM((CHUNKS, N_CTX, 64, WIDTH), BF16),
             pltpu.VMEM((CHUNKS, N_CTX, 64, WIDTH), BF16),
             pltpu.VMEM((CHUNKS, N_DP, ROWS, WIDTH), BF16),
-            pltpu.VMEM((CHUNKS, N_DP, ROWS, WIDTH), BF16),
             pltpu.VMEM((N_DP, ROWS, N_DP * ROWS), BF16),
             pltpu.VMEM((CHUNKS, N_DP * ROWS, WIDTH), BF16),
             pltpu.VMEM((N_DP, STATE, N_DP * ROWS), BF16),
@@ -457,6 +494,7 @@
             pltpu.VMEM((N_DP, ROWS), F32),
             pltpu.VMEM((N_DP, ROWS, 128), F32),
             pltpu.VMEM((2, CHUNKS, 128, WIDTH), BF16),
+            dma((4,)),
             dma((4 + CHUNKS,)),
             dma((4,)),
             dma((4,)),
@@ -470,12 +508,38 @@
             dma((CHUNKS,)),
         ],
         compiler_params=pltpu.CompilerParams(
-            collective_id=0, has_side_effects=True, vmem_limit_bytes=60 * 2**20
+            collective_id=0, has_side_effects=True, vmem_limit_bytes=54 * 2**20
         ),
         cost_estimate=pl.CostEstimate(
             flops=14 * 10**9, bytes_accessed=16 * 2**20, transcendentals=4 * 10**6
         ),
-    )(ssm_input, gate_input, write_basis, read_basis, packet, rates, skips, gains)
+    )(
+        ssm_input,
+        write_basis,
+        read_basis,
+        step_size,
+        row_owner.reshape(1, -1),
+        document_lengths,
+        decay_rate.reshape(1, -1),
+        skip_weight.reshape(1, -1),
+    )
+    return pl.pallas_call(
+        finish,
+        out_shape=jax.ShapeDtypeStruct((ROWS, GROUPS * 1024), BF16),
+        in_specs=[anywhere, anywhere, vmem],
+        out_specs=anywhere,
+        scratch_shapes=[
+            pltpu.VMEM((GROUPS, ROWS, 1024), BF16),
+            pltpu.VMEM((GROUPS, ROWS, 1024), BF16),
+            pltpu.VMEM((GROUPS, ROWS, 1024), BF16),
+            dma((2, GROUPS)),
+            dma((GROUPS,)),
+        ],
+        compiler_params=pltpu.CompilerParams(vmem_limit_bytes=54 * 2**20),
+        cost_estimate=pl.CostEstimate(
+            flops=20 * 2**20, bytes_accessed=12 * 2**20, transcendentals=2 * 2**20
+        ),
+    )(mixed, gate_input, norm_gain.reshape(1, -1))
 
 
 def solution(mesh):

time: 134 us -> 122 us (0.910)
  local copies, waits for them, and re-layouts: 7.65 us -> 0 us
  other arithmetic: 2.95 us -> 0 us
    pallas_call x1, Pallas kernels: 122 us -> 114 us  [shards(): pl.pallas_call(kernel, out_shape=jax.ShapeDtypeStruct((ROWS, GROUPS * 102...]
    pallas_call x0 -> x1, Pallas kernels: none -> 6.79 us  [shards(): pl.pallas_call(finish, out_shape=jax.ShapeDtypeStruct((ROWS, GROUPS * 102...]
    unnamed x1 -> x0, local copies, waits for them, and re-layouts: 4.64 us -> none
    broadcast_in_dim x6 -> x0, local copies, waits for them, and re-layouts: 1.51 us -> none  [the longest x3 1.5 us: shards(): skips = jnp.repeat(skip_weight, 64).reshape(GROUPS, 1024)]
    reshape x2 -> x0, local copies, waits for them, and re-layouts: 1.42 us -> none  [the longest x1 1.32 us: shards(): rates = decay_rate.reshape(GROUPS, HEADS)]
where the time goes in v2:
time: 122 us; the launch traced here: 121 us
  Pallas kernels  121 us (99%)
    pallas_call x1, Pallas kernels, shards(): pl.pallas_call(kernel, out_shape=jax.ShapeDtypeStruct((ROWS, GROUPS * 102...  114 us
    pallas_call x1, Pallas kernels, shards(): pl.pallas_call(finish, out_shape=jax.ShapeDtypeStruct((ROWS, GROUPS * 102...  6.79 us

profile of v2, /device:TPU:1, one launch (start us, length us, event | category | flops | bytes accessed | tf_op | source)
XLA Modules:
  0.0 121.1 jit_solution(12816343995242601218)
XLA Ops:
  0.0 114.3 %shard_map.100.mixed_hbm = bf16[256,8192]{1,0:T(8,128)(2,1)} custom-call(bf16[256,8192]{1,0:T(8,128)(2,1)} %x_ref.1, bf16[256,1024]{1,0:T(8,128)(2,1)} %write_ref.1, bf16[256,1024]{1,0:T(8,128)(2,1)} %read_ref.1, bf16[256,128]{1,0:T(8,128)(2,1)} %step_ref.1, s32[1,256]{1,0:T(1,128)} %bitcast.5, s32[1,8]{1,0:T(1,128)} %length_hbm.1, f32[1,128]{1,0:T(1,128)} %bitcast.6, ...), custom_call_target="tpu_custom_call" | custom-call | flops 14000000000 | bytes 16777216 | tf_op jit(solution)/shard_map/pallas_call | solution.py:465
  114.3 6.8 %shard_map.101 = bf16[256,8192]{1,0:T(8,128)(2,1)} custom-call(bf16[256,8192]{1,0:T(8,128)(2,1)} %shard_map.100.mixed_hbm, bf16[256,8192]{1,0:T(8,128)(2,1)} %gate_hbm.1, f32[1,8192]{1,0:T(1,128)} %bitcast.4), custom_call_target="tpu_custom_call" | custom-call | flops 20971520 | bytes 12582912 | tf_op jit(solution)/shard_map/pallas_call | solution.py:526

commit v3 on v2

--- a/solution.py
+++ b/solution.py
@@ -37,6 +37,10 @@
     return high, middle, low
 
 
+def silu(value):
+    return value / (1.0 + jnp.exp(-value))
+
+
 def iota(shape, dim):
     return lax.broadcasted_iota(jnp.int32, shape, dim)
 
@@ -50,7 +54,13 @@
     length_hbm,
     rate_hbm,
     skip_hbm,
-    out_ref,
+    gate_hbm,
+    gated_ref,
+    squares_ref,
+    last_ref,
+    gates,
+    landed,
+    squares,
     owner_ref,
     length_ref,
     rate_ref,
@@ -77,6 +87,9 @@
     keys_row,
     keys_col,
     spread,
+    inner,
+    gate_sem,
+    done_sem,
     small_sem,
     local_sem,
     send_sem,
@@ -134,7 +147,8 @@
         pltpu.make_async_copy(rate_hbm, rate_ref, small_sem.at[2]),
         pltpu.make_async_copy(skip_hbm, skip_ref, small_sem.at[3]),
     ]
-    for copy in own[:1] + small + own[1:] + own_x:
+    gate_copy = pltpu.make_async_copy(gate_hbm, gates, gate_sem.at[0])
+    for copy in own[:1] + small + own[1:] + own_x + [gate_copy]:
         copy.start()
     pl.semaphore_wait(barrier, N_DP + N_CTX - 2)
 
@@ -287,7 +301,10 @@
         flipped = writes[i].astype(F32).T
         for k in range(N_DP):
             kept = keys_row[i : i + 1, :] == key_end[k : k + 1, :]
-            writes_t[k, :, i * ROWS : (i + 1) * ROWS] = jnp.where(kept, flipped, 0.0).astype(BF16)
+            half = pl.ds((k % 2) * STATE, STATE)
+            writes_t[k // 2, half, i * ROWS : (i + 1) * ROWS] = jnp.where(
+                kept, flipped, 0.0
+            ).astype(BF16)
     own[2].wait()
     arrived(reads, N_DP - 1, recv_sem.at[2])
 
@@ -329,13 +346,14 @@
         lax.fori_loop(0, N_DP, scale, 0)
 
         def collect(k, carry):
-            k = lax.rem(k + col // 2, N_DP)
-            part = dot(writes_t[k], scaled[c])
-            half = aux[k, 1:2, pl.ds(pl.multiple_of(c * WIDTH, WIDTH), WIDTH)]
-            part = (part * half).astype(BF16)
-            for side in range(2):
-                peer = 2 * k + side
-                sums[c, peer] = part[64 * side : 64 * side + 64]
+            pair = lax.rem(k + col // 4, N_DP // 2)
+            part = dot(writes_t[pair], scaled[c])
+            for side in range(4):
+                peer = 4 * pair + side
+                half = aux[
+                    2 * pair + side // 2, 1:2, pl.ds(pl.multiple_of(c * WIDTH, WIDTH), WIDTH)
+                ]
+                sums[c, peer] = (part[64 * side : 64 * side + 64] * half).astype(BF16)
 
                 @pl.when(peer != col)
                 def _():
@@ -345,7 +363,7 @@
 
             return carry
 
-        lax.fori_loop(0, N_DP, collect, 0)
+        lax.fori_loop(0, N_DP // 2, collect, 0)
         sums_in[c, col] = sums[c, col]
 
     def carry_on(c):
@@ -373,22 +391,35 @@
             mixed.at[c, peer], piece(out_ref, me, c), y_send.at[c], y_recv.at[c], "dp", peer
         ).start()
 
+    def look_back(c):
+        for i in range(N_DP):
+            reach = (i + 1) * ROWS
+            inner[c, i] = dot(scores[i, :, 0:reach], scaled[c, 0:reach, :])
+
     def mix(c):
         arrived(states_in.at[c], N_CTX - 1, h_recv.at[c])
-
         carried = states_in[c].reshape(N_DP * STATE, WIDTH)
         skip = skips[c, 0:1, :]
         for i in range(N_DP):
-            reach = (i + 1) * ROWS
-            both = dot(scores[i, :, 0:reach], scaled[c, 0:reach, :]) + dot(reads_m[i], carried)
+            both = inner[c, i] + dot(reads_m[i], carried)
             factor = dot(factors[i], spread[0, c])
             mixed[c, i] = (both * factor + skip * xs[c, i].astype(F32)).astype(BF16)
 
-            @pl.when(me != i)
+            @pl.when((me != i) & (c < CHUNKS - 1))
             def _():
-                hand_back(c, i)
-
-        pltpu.make_async_copy(mixed.at[c, me], piece(out_ref, me, c), local_sem.at[3]).start()
+                remote(
+                    mixed.at[c, i], landed.at[c, me], y_send.at[c], y_recv.at[c], "dp", i
+                ).start()
+
+            @pl.when((me != i) & (c == CHUNKS - 1))
+            def _():
+                remote(
+                    mixed.at[c, i], last_ref.at[me], y_send.at[c], y_recv.at[c], "dp", i
+                ).start()
+
+        @pl.when(c < CHUNKS - 1)
+        def _():
+            landed[c, me] = mixed[c, me]
 
     def step(s, carry):
         @pl.when(s < CHUNKS)
@@ -403,13 +434,41 @@
         def _():
             mix(s - 2)
 
+        @pl.when(s < CHUNKS)
+        def _():
+            look_back(s)
+
         return carry
 
     lax.fori_loop(0, CHUNKS + 2, step, 0)
 
-    arrived(mixed.at[0], CHUNKS, local_sem.at[3])
-    for c in range(CHUNKS):
-        arrived(mixed.at[c], N_DP - 1, y_recv.at[c])
+    last_copy = pltpu.make_async_copy(
+        mixed.at[CHUNKS - 1, me], last_ref.at[me], local_sem.at[3]
+    )
+    last_copy.start()
+    gate_copy.wait()
+    squares[...] = jnp.zeros((ROWS, 128), F32)
+    results = []
+    for c in range(CHUNKS - 1):
+        arrived(landed.at[c], N_DP - 1, y_recv.at[c])
+
+        def gating(g, carry):
+            gate = gates[:, pl.ds(pl.multiple_of(g * 1024 + c * WIDTH, WIDTH), WIDTH)].astype(F32)
+            gated = landed[c, g].astype(F32) * silu(gate)
+            landed[c, g] = gated.astype(BF16)
+            total = jnp.sum(gated * gated, axis=1, keepdims=True)
+            squares[...] += jnp.where(iota((ROWS, 128), 1) == g, total, 0.0)
+            return carry
+
+        lax.fori_loop(0, GROUPS, gating, 0)
+        results.append(pltpu.make_async_copy(landed.at[c], gated_ref.at[c], done_sem.at[c]))
+        results[-1].start()
+    results.append(pltpu.make_async_copy(squares, squares_ref, done_sem.at[CHUNKS - 1]))
+    results[-1].start()
+    for copy in results:
+        copy.wait()
+    last_copy.wait()
+    arrived(mixed.at[CHUNKS - 1], N_DP - 1, y_recv.at[CHUNKS - 1])
 
     arrived(meta, N_DP - 1, send_sem.at[0])
     arrived(writes, N_DP - 1, send_sem.at[1])
@@ -422,28 +481,56 @@
         arrived(mixed.at[c], N_DP - 1, y_send.at[c])
 
 
-def finish(mixed_hbm, gate_hbm, gain_ref, out_ref, mixed, gates, done, load_sem, done_sem):
-    def part(ref, g):
-        return ref.at[:, pl.ds(pl.multiple_of(g * 1024, 1024), 1024)]
+def finish(
+    gated_hbm,
+    squares_ref,
+    last_hbm,
+    gate_hbm,
+    gain_ref,
+    out_ref,
+    gated,
+    lasts,
+    gates,
+    done,
+    load_sem,
+    done_sem,
+):
+    early = WIDTH * (CHUNKS - 1)
+
+    def loads(g):
+        start = pl.multiple_of(g * 1024 + early, WIDTH)
+        return [
+            pltpu.make_async_copy(gate_hbm.at[:, pl.ds(start, WIDTH)], gates.at[g], load_sem.at[0, g]),
+            pltpu.make_async_copy(last_hbm.at[g], lasts.at[g], load_sem.at[1, g]),
+            pltpu.make_async_copy(gated_hbm.at[:, g], gated.at[g], load_sem.at[2, g]),
+        ]
+
+    def result(g):
+        place = pl.ds(pl.multiple_of(g * 1024, 1024), 1024)
+        return pltpu.make_async_copy(done.at[g], out_ref.at[:, place], done_sem.at[g])
 
     for g in range(GROUPS):
-        pltpu.make_async_copy(part(gate_hbm, g), gates.at[g], load_sem.at[0, g]).start()
-        pltpu.make_async_copy(part(mixed_hbm, g), mixed.at[g], load_sem.at[1, g]).start()
+        for copy in loads(g):
+            copy.start()
 
     def group(g, carry):
-        pltpu.make_async_copy(part(gate_hbm, g), gates.at[g], load_sem.at[0, g]).wait()
-        pltpu.make_async_copy(part(mixed_hbm, g), mixed.at[g], load_sem.at[1, g]).wait()
-        gate = gates[g].astype(F32)
-        gated = mixed[g].astype(F32) * (gate / (1.0 + jnp.exp(-gate)))
-        inverse = lax.rsqrt(jnp.mean(gated * gated, axis=1, keepdims=True) + EPSILON)
-        gain = gain_ref[:, pl.ds(pl.multiple_of(g * 1024, 1024), 1024)]
-        done[g] = (gated * inverse * gain).astype(BF16)
-        pltpu.make_async_copy(done.at[g], part(out_ref, g), done_sem.at[g]).start()
+        for copy in loads(g):
+            copy.wait()
+        late = lasts[g].astype(F32) * silu(gates[g].astype(F32))
+        total = jnp.where(iota((ROWS, 128), 1) == g, squares_ref[...], 0.0)
+        for k in range(WIDTH // 128):
+            total = total + late[:, k * 128 : (k + 1) * 128] * late[:, k * 128 : (k + 1) * 128]
+        inverse = lax.rsqrt(jnp.sum(total, axis=1, keepdims=True) * (1.0 / 1024.0) + EPSILON)
+        for c in range(CHUNKS):
+            part = gated[g, c].astype(F32) if c < CHUNKS - 1 else late
+            gain = gain_ref[:, pl.ds(pl.multiple_of(g * 1024 + c * WIDTH, WIDTH), WIDTH)]
+            done[g, :, c * WIDTH : (c + 1) * WIDTH] = (part * inverse * gain).astype(BF16)
+        result(g).start()
         return carry
 
     lax.fori_loop(0, GROUPS, group, 0)
     for g in range(GROUPS):
-        pltpu.make_async_copy(done.at[g], part(out_ref, g), done_sem.at[g]).wait()
+        result(g).wait()
 
 
 def shards(
@@ -462,12 +549,19 @@
     anywhere = pl.BlockSpec(memory_space=pl.ANY)
     vmem = pl.BlockSpec(memory_space=pltpu.VMEM)
     dma = pltpu.SemaphoreType.DMA
-    mixed = pl.pallas_call(
+    gated, squares, last = pl.pallas_call(
         kernel,
-        out_shape=jax.ShapeDtypeStruct((ROWS, GROUPS * 1024), BF16),
-        in_specs=[hbm] * 8,
-        out_specs=anywhere,
+        out_shape=[
+            jax.ShapeDtypeStruct((CHUNKS - 1, GROUPS, ROWS, WIDTH), BF16),
+            jax.ShapeDtypeStruct((ROWS, 128), F32),
+            jax.ShapeDtypeStruct((GROUPS, ROWS, WIDTH), BF16),
+        ],
+        in_specs=[hbm] * 9,
+        out_specs=[anywhere] * 3,
         scratch_shapes=[
+            pltpu.VMEM((ROWS, GROUPS * 1024), BF16),
+            pltpu.VMEM((CHUNKS - 1, N_DP, ROWS, WIDTH), BF16),
+            pltpu.VMEM((ROWS, 128), F32),
             pltpu.VMEM((1, ROWS), jnp.int32),
             pltpu.VMEM((1, DOCS), jnp.int32),
             pltpu.VMEM((1, 128), F32),
@@ -488,12 +582,15 @@
             pltpu.VMEM((CHUNKS, N_DP, ROWS, WIDTH), BF16),
             pltpu.VMEM((N_DP, ROWS, N_DP * ROWS), BF16),
             pltpu.VMEM((CHUNKS, N_DP * ROWS, WIDTH), BF16),
-            pltpu.VMEM((N_DP, STATE, N_DP * ROWS), BF16),
+            pltpu.VMEM((N_DP // 2, 2 * STATE, N_DP * ROWS), BF16),
             pltpu.VMEM((N_DP, ROWS, N_DP * STATE), BF16),
             pltpu.VMEM((N_DP, ROWS, 128), BF16),
             pltpu.VMEM((N_DP, ROWS), F32),
             pltpu.VMEM((N_DP, ROWS, 128), F32),
             pltpu.VMEM((2, CHUNKS, 128, WIDTH), BF16),
+            pltpu.VMEM((CHUNKS, N_DP, ROWS, WIDTH), F32),
+            dma((1,)),
+            dma((CHUNKS,)),
             dma((4,)),
             dma((4 + CHUNKS,)),
             dma((4,)),
@@ -508,7 +605,7 @@
             dma((CHUNKS,)),
         ],
         compiler_params=pltpu.CompilerParams(
-            collective_id=0, has_side_effects=True, vmem_limit_bytes=54 * 2**20
+            collective_id=0, has_side_effects=True, vmem_limit_bytes=60 * 2**20
         ),
         cost_estimate=pl.CostEstimate(
             flops=14 * 10**9, bytes_accessed=16 * 2**20, transcendentals=4 * 10**6
@@ -522,24 +619,26 @@
         document_lengths,
         decay_rate.reshape(1, -1),
         skip_weight.reshape(1, -1),
+        gate_input,
     )
     return pl.pallas_call(
         finish,
         out_shape=jax.ShapeDtypeStruct((ROWS, GROUPS * 1024), BF16),
-        in_specs=[anywhere, anywhere, vmem],
+        in_specs=[anywhere, vmem, anywhere, anywhere, vmem],
         out_specs=anywhere,
         scratch_shapes=[
+            pltpu.VMEM((GROUPS, CHUNKS - 1, ROWS, WIDTH), BF16),
+            pltpu.VMEM((GROUPS, ROWS, WIDTH), BF16),
+            pltpu.VMEM((GROUPS, ROWS, WIDTH), BF16),
             pltpu.VMEM((GROUPS, ROWS, 1024), BF16),
-            pltpu.VMEM((GROUPS, ROWS, 1024), BF16),
-            pltpu.VMEM((GROUPS, ROWS, 1024), BF16),
-            dma((2, GROUPS)),
+            dma((3, GROUPS)),
             dma((GROUPS,)),
         ],
-        compiler_params=pltpu.CompilerParams(vmem_limit_bytes=54 * 2**20),
+        compiler_params=pltpu.CompilerParams(vmem_limit_bytes=60 * 2**20),
         cost_estimate=pl.CostEstimate(
             flops=20 * 2**20, bytes_accessed=12 * 2**20, transcendentals=2 * 2**20
         ),
-    )(mixed, gate_input, norm_gain.reshape(1, -1))
+    )(gated, squares, last, gate_input, norm_gain.reshape(1, -1))
 
 
 def solution(mesh):

time: 122 us -> 120 us (0.984)
    pallas_call x1, Pallas kernels: 6.79 us -> 5.37 us  [shards(): pl.pallas_call(finish, out_shape=jax.ShapeDtypeStruct((ROWS, GROUPS * 102...]
where the time goes in v3:
time: 120 us
  Pallas kernels  120 us (100%)
    pallas_call x1, Pallas kernels, shards(): pl.pallas_call(kernel, out_shape=[jax.ShapeDtypeStruct((CHUNKS - 1, GROUP...  114 us
    pallas_call x1, Pallas kernels, shards(): pl.pallas_call(finish, out_shape=jax.ShapeDtypeStruct((ROWS, GROUPS * 102...  5.37 us

profile of v3, /device:TPU:1, one launch (start us, length us, event | category | flops | bytes accessed | tf_op | source)
XLA Modules:
  0.0 119.7 jit_solution(9555337535026372998)
XLA Ops:
  0.0 114.3 %shard_map.100 = (bf16[3,8,256,256]{3,2,1,0:T(8,128)(2,1)}, f32[256,128]{1,0:T(8,128)}, bf16[8,256,256]{2,1,0:T(8,128)(2,1)}) custom-call(bf16[256,8192]{1,0:T(8,128)(2,1)} %x_ref.1, bf16[256,1024]{1,0:T(8,128)(2,1)} %write_ref.1, bf16[256,1024]{1,0:T(8,128)(2,1)} %read_ref.1, bf16[256,128]{1,0:T(8,128)(2,1)} %step_ref.1, s32[1,256]{1,0:T(1,128)} %bitcast.5, ...), custom_call_target="tpu_custom_call" | custom-call | flops 14000000000 | bytes 16777216 | tf_op jit(solution)/shard_map/pallas_call | solution.py:552
  114.3 5.4 %shard_map.101 = bf16[256,8192]{1,0:T(8,128)(2,1)} custom-call(bf16[3,8,256,256]{3,2,1,0:T(8,128)(2,1)} %get-tuple-element.8.gated_hbm, f32[256,128]{1,0:T(8,128)} %get-tuple-element.9.squares_ref, bf16[8,256,256]{2,1,0:T(8,128)(2,1)} %get-tuple-element.10.last_hbm, bf16[256,8192]{1,0:T(8,128)(2,1)} %gate_hbm.3, f32[1,8192]{1,0:T(1,128)} %bitcast.4), custom_call_target="tpu_custom_call" | custom-call | flops 20971520 | bytes 12582912 | tf_op jit(solution)/shard_map/pallas_call | solution.py:624

commit v4 on v3

--- a/solution.py
+++ b/solution.py
@@ -174,17 +174,18 @@
     own[0].wait()
     for copy in small:
         copy.wait()
-    packet[:, 0:HEADS, :] = steps[...].astype(F32).T.reshape(GROUPS, HEADS, ROWS).astype(BF16)
+    packet[:, :, 0:ROWS] = steps[...].astype(F32).T.reshape(GROUPS, HEADS, ROWS).astype(BF16)
     owner_row = owner_ref[...].astype(F32)
-    line = iota((16, ROWS), 0)
-    lane = iota((16, ROWS), 1)
-    extra = jnp.where(line == 0, owner_row, 0.0)
+    line = iota((HEADS, 128), 0)
+    lane = iota((HEADS, 128), 1)
+    extra = jnp.where(line == 0, owner_row[:, 0:128], 0.0)
+    extra = jnp.where(line == 1, owner_row[:, 128:256], extra)
     for d in range(DOCS):
         length = length_ref[0:1, d : d + 1]
-        extra = jnp.where((line == 1) & (lane == d), (length // 64).astype(F32), extra)
-        extra = jnp.where((line == 2) & (lane == d), (length % 64).astype(F32), extra)
+        extra = jnp.where((line == 2) & (lane == d), (length // 64).astype(F32), extra)
+        extra = jnp.where((line == 3) & (lane == d), (length % 64).astype(F32), extra)
     for k in range(GROUPS):
-        packet[k, 16:32, :] = extra.astype(BF16)
+        packet[k, :, ROWS : ROWS + 128] = extra.astype(BF16)
     for d in range(1, N_DP):
         peer = lax.rem(me + d, N_DP)
         remote(
@@ -214,9 +215,9 @@
     arrived(meta, N_DP - 1, recv_sem.at[0])
     first_slot = (col * BLOCK).astype(F32)
 
-    extras = meta[:, 16:32, :].astype(F32)
-    owners = extras[:, 0, :]
-    lengths = extras[:, 1, :] * 64.0 + extras[:, 2, :]
+    extras = meta[:, :, ROWS : ROWS + 128].astype(F32)
+    owners = jnp.concatenate([extras[:, 0, :], extras[:, 1, :]], axis=1)
+    lengths = extras[:, 2, :] * 64.0 + extras[:, 3, :]
     starts = []
     total = jnp.zeros((N_DP, 1), F32)
     for d in range(DOCS):
@@ -263,7 +264,7 @@
     running = []
     for i in range(N_DP):
         keys_col[i] = jnp.broadcast_to(key_t[:, i : i + 1], (ROWS, 128))
-        step = meta[i, 0:HEADS, :]
+        step = meta[i, :, 0:ROWS]
         owned = table[i]
         same = jnp.where((owner_t[:, i : i + 1] == owners[i : i + 1, :]) & not_later, 1.0, 0.0)
         running.append(dot(step, same.astype(BF16)) + exact(sofar, owned))
@@ -272,7 +273,7 @@
     middle = -0.5 * rate * sofar
     for i in range(N_DP):
         exponent = -rate * running[i] - exact(middle, table[i])
-        rising = thirds(jnp.exp(-exponent) * meta[i, 0:HEADS, :].astype(F32))
+        rising = thirds(jnp.exp(-exponent) * meta[i, :, 0:ROWS].astype(F32))
         falling = thirds(jnp.exp(exponent))
         stack = jnp.concatenate(falling + rising + (jnp.zeros((32, ROWS), F32),), axis=0)
         factors[i] = stack.T.astype(BF16)
@@ -567,9 +568,9 @@
             pltpu.VMEM((1, 128), F32),
             pltpu.VMEM((1, 128), F32),
             pltpu.VMEM((ROWS, 128), BF16),
-            pltpu.VMEM((N_DP, 32, ROWS), BF16),
+            pltpu.VMEM((N_DP, HEADS, ROWS + 128), BF16),
             pltpu.VMEM((CHUNKS, 8, WIDTH), F32),
-            pltpu.VMEM((N_DP, 32, ROWS), BF16),
+            pltpu.VMEM((N_DP, HEADS, ROWS + 128), BF16),
             pltpu.VMEM((N_DP, ROWS, STATE), BF16),
             pltpu.VMEM((N_DP, ROWS, STATE), BF16),
             pltpu.VMEM((CHUNKS, N_DP, ROWS, WIDTH), BF16),

time: 120 us -> 119 us (level)
  no operation moved by 1% of the time
where the time goes in v4:
time: 119 us
  Pallas kernels  119 us (100%)
    pallas_call x1, Pallas kernels, shards(): pl.pallas_call(kernel, out_shape=[jax.ShapeDtypeStruct((CHUNKS - 1, GROUP...  114 us
    pallas_call x1, Pallas kernels, shards(): pl.pallas_call(finish, out_shape=jax.ShapeDtypeStruct((ROWS, GROUPS * 102...  5.37 us

profile of v4, /device:TPU:1, one launch (start us, length us, event | category | flops | bytes accessed | tf_op | source)
XLA Modules:
  0.0 119.3 jit_solution(5527713267550414482)
XLA Ops:
  0.0 114.0 %shard_map.100 = (bf16[3,8,256,256]{3,2,1,0:T(8,128)(2,1)}, f32[256,128]{1,0:T(8,128)}, bf16[8,256,256]{2,1,0:T(8,128)(2,1)}) custom-call(bf16[256,8192]{1,0:T(8,128)(2,1)} %x_ref.1, bf16[256,1024]{1,0:T(8,128)(2,1)} %write_ref.1, bf16[256,1024]{1,0:T(8,128)(2,1)} %read_ref.1, bf16[256,128]{1,0:T(8,128)(2,1)} %step_ref.1, s32[1,256]{1,0:T(1,128)} %bitcast.5, ...), custom_call_target="tpu_custom_call" | custom-call | flops 14000000000 | bytes 16777216 | tf_op jit(solution)/shard_map/pallas_call | solution.py:553
  114.0 5.4 %shard_map.101 = bf16[256,8192]{1,0:T(8,128)(2,1)} custom-call(bf16[3,8,256,256]{3,2,1,0:T(8,128)(2,1)} %get-tuple-element.8.gated_hbm, f32[256,128]{1,0:T(8,128)} %get-tuple-element.9.squares_ref, bf16[8,256,256]{2,1,0:T(8,128)(2,1)} %get-tuple-element.10.last_hbm, bf16[256,8192]{1,0:T(8,128)(2,1)} %gate_hbm.3, f32[1,8192]{1,0:T(1,128)} %bitcast.4), custom_call_target="tpu_custom_call" | custom-call | flops 20971520 | bytes 12582912 | tf_op jit(solution)/shard_map/pallas_call | solution.py:625

commit v5 on v4

--- a/solution.py
+++ b/solution.py
@@ -148,7 +148,7 @@
         pltpu.make_async_copy(skip_hbm, skip_ref, small_sem.at[3]),
     ]
     gate_copy = pltpu.make_async_copy(gate_hbm, gates, gate_sem.at[0])
-    for copy in own[:1] + small + own[1:] + own_x + [gate_copy]:
+    for copy in own[:1] + small:
         copy.start()
     pl.semaphore_wait(barrier, N_DP + N_CTX - 2)
 
@@ -198,6 +198,9 @@
             remote(
                 piece(x_ref, peer, c), xs.at[c, me], x_send.at[c], x_recv.at[c], "dp", peer
             ).start()
+
+    for copy in own[1:] + own_x + [gate_copy]:
+        copy.start()
 
     row = iota((128, WIDTH), 0)
     for c in range(CHUNKS):
@@ -484,15 +487,18 @@
 
 def finish(
     gated_hbm,
-    squares_ref,
+    squares_hbm,
     last_hbm,
     gate_hbm,
+    gain_hbm,
+    out_ref,
+    squares_ref,
     gain_ref,
-    out_ref,
     gated,
     lasts,
     gates,
     done,
+    row_sem,
     load_sem,
     done_sem,
 ):
@@ -510,9 +516,17 @@
         place = pl.ds(pl.multiple_of(g * 1024, 1024), 1024)
         return pltpu.make_async_copy(done.at[g], out_ref.at[:, place], done_sem.at[g])
 
-    for g in range(GROUPS):
+    shared = [
+        pltpu.make_async_copy(squares_hbm, squares_ref, row_sem.at[0]),
+        pltpu.make_async_copy(gain_hbm, gain_ref, row_sem.at[1]),
+    ]
+    for copy in loads(0) + shared:
+        copy.start()
+    for g in range(1, GROUPS):
         for copy in loads(g):
             copy.start()
+    for copy in shared:
+        copy.wait()
 
     def group(g, carry):
         for copy in loads(g):
@@ -548,7 +562,6 @@
 ):
     hbm = pl.BlockSpec(memory_space=pltpu.HBM)
     anywhere = pl.BlockSpec(memory_space=pl.ANY)
-    vmem = pl.BlockSpec(memory_space=pltpu.VMEM)
     dma = pltpu.SemaphoreType.DMA
     gated, squares, last = pl.pallas_call(
         kernel,
@@ -625,13 +638,16 @@
     return pl.pallas_call(
         finish,
         out_shape=jax.ShapeDtypeStruct((ROWS, GROUPS * 1024), BF16),
-        in_specs=[anywhere, vmem, anywhere, anywhere, vmem],
+        in_specs=[anywhere] * 5,
         out_specs=anywhere,
         scratch_shapes=[
+            pltpu.VMEM((ROWS, 128), F32),
+            pltpu.VMEM((1, GROUPS * 1024), F32),
             pltpu.VMEM((GROUPS, CHUNKS - 1, ROWS, WIDTH), BF16),
             pltpu.VMEM((GROUPS, ROWS, WIDTH), BF16),
             pltpu.VMEM((GROUPS, ROWS, WIDTH), BF16),
             pltpu.VMEM((GROUPS, ROWS, 1024), BF16),
+            dma((2,)),
             dma((3, GROUPS)),
             dma((GROUPS,)),
         ],

time: 119 us -> 119 us (level)
  no operation moved by 1% of the time
where the time goes in v5:
time: 119 us
  Pallas kernels  119 us (100%)
    pallas_call x1, Pallas kernels, shards(): pl.pallas_call(kernel, out_shape=[jax.ShapeDtypeStruct((CHUNKS - 1, GROUP...  114 us
    pallas_call x1, Pallas kernels, shards(): pl.pallas_call(finish, out_shape=jax.ShapeDtypeStruct((ROWS, GROUPS * 102...  5.33 us

profile of v5, /device:TPU:1, one launch (start us, length us, event | category | flops | bytes accessed | tf_op | source)
XLA Modules:
  0.0 119.3 jit_solution(6798578125865712146)
XLA Ops:
  0.0 114.0 %shard_map.100 = (bf16[3,8,256,256]{3,2,1,0:T(8,128)(2,1)}, f32[256,128]{1,0:T(8,128)}, bf16[8,256,256]{2,1,0:T(8,128)(2,1)}) custom-call(bf16[256,8192]{1,0:T(8,128)(2,1)} %x_ref.1, bf16[256,1024]{1,0:T(8,128)(2,1)} %write_ref.1, bf16[256,1024]{1,0:T(8,128)(2,1)} %read_ref.1, bf16[256,128]{1,0:T(8,128)(2,1)} %step_ref.1, s32[1,256]{1,0:T(1,128)} %bitcast.5, ...), custom_call_target="tpu_custom_call" | custom-call | flops 14000000000 | bytes 16777216 | tf_op jit(solution)/shard_map/pallas_call | solution.py:566
  114.0 5.3 %shard_map.101 = bf16[256,8192]{1,0:T(8,128)(2,1)} custom-call(bf16[3,8,256,256]{3,2,1,0:T(8,128)(2,1)} %get-tuple-element.8.gated_hbm, f32[256,128]{1,0:T(8,128)} %get-tuple-element.9.squares_hbm, bf16[8,256,256]{2,1,0:T(8,128)(2,1)} %get-tuple-element.10.last_hbm, bf16[256,8192]{1,0:T(8,128)(2,1)} %gate_hbm.3, f32[1,8192]{1,0:T(1,128)} %bitcast.4), custom_call_target="tpu_custom_call" | custom-call | flops 20971520 | bytes 12582912 | tf_op jit(solution)/shard_map/pallas_call | solution.py:638
